TPU v7x, 256 devices: a whole 4x4x8 slice. The times are simulated.
256 devices in a mesh: row: 8 (over y_hi, x), col: 16 (over y_lo, z), rep: 2 (over core).
Axes of the slice: x: 4, y: 4 (y_hi: 2, y_lo: 2; y = y_hi * 2 + y_lo), z: 8, core: 2. Of those that a mesh axis runs over, the one named last changes fastest.
Arguments:
- tokens: bfloat16 [4096, 5120], P(('col', 'rep'), 'row'), may hold values from -6 to 6
- out_grad: bfloat16 [4096, 5120], P(('col', 'rep'), 'row'), may hold values from -6 to 6
- w_in: bfloat16 [5120, 13824], P('row', 'col'), may hold values from -0.078125 to 0.078125
- bias_in: float32 [13824], P('col'), may hold values from -3 to 3
- w_out: bfloat16 [13824, 5120], P('col', 'row'), may hold values from -0.0546875 to 0.0546875
Outputs:
- input_grad: bfloat16 [4096, 5120], P(('col', 'rep'), 'row')
- w_in_grad: bfloat16 [5120, 13824], P('row', ('col', 'rep'))
- bias_grad: float32 [13824], P(('col', 'rep'))
- w_out_grad: bfloat16 [13824, 5120], P(('col', 'rep'), 'row')
All inputs are finite; a program needn't handle non-finite values.
Results may differ from a plain program's by a relative error of at most 0.03.
Values may be sent and summed in bfloat16 or wider, within the bound.
A program may use at most 64 MiB of HBM per device.

v0:
```python
import jax
import jax.numpy as jnp
from jax import lax
from jax.sharding import PartitionSpec as P


def act_fn(value):
    return jax.nn.gelu(value, approximate=True)


def local(tokens, out_grad, w_in, bias_in, w_out):
    rows_x, rows_g = (
        lax.all_gather(tokens, "col", axis=0, tiled=True),
        lax.all_gather(out_grad, "col", axis=0, tiled=True),
    )
    piece = rows_x
    pre_sum = lax.psum_scatter(
        jnp.dot(piece, w_in, preferred_element_type=jnp.float32).astype(jnp.bfloat16),
        "row",
        scatter_dimension=0,
        tiled=True,
    ).astype(jnp.float32)
    piece = rows_g
    back_sum = lax.psum_scatter(
        lax.dot_general(
            piece, w_out, (((1,), (1,)), ((), ())), preferred_element_type=jnp.float32
        ).astype(jnp.bfloat16),
        "row",
        scatter_dimension=0,
        tiled=True,
    ).astype(jnp.float32)
    activation, pullback = jax.vjp(act_fn, pre_sum + bias_in[None, :])
    act_local = activation.astype(jnp.bfloat16)
    grad_local = pullback(back_sum)[0].astype(jnp.bfloat16)
    act_rows, grad_rows = (
        lax.all_gather(act_local, "row", axis=0, tiled=True),
        lax.all_gather(grad_local, "row", axis=0, tiled=True),
    )
    total_tokens = rows_x.shape[0] * lax.axis_size("rep")
    factor = 1.0 / jnp.sqrt(jnp.float32(total_tokens))
    w_in_part = (
        lax.dot_general(
            rows_x, grad_rows, (((0,), (0,)), ((), ())), preferred_element_type=jnp.float32
        )
        * factor
    )
    w_out_part = (
        lax.dot_general(
            act_rows, rows_g, (((0,), (0,)), ((), ())), preferred_element_type=jnp.float32
        )
        * factor
    )
    bias_part = jnp.sum(grad_rows.astype(jnp.float32), axis=0) * factor
    w_in_sum, w_out_sum, bias_sum = (
        lax.psum_scatter(
            w_in_part.astype(jnp.bfloat16), "rep", scatter_dimension=1, tiled=True
        ).astype(jnp.float32),
        lax.psum_scatter(
            w_out_part.astype(jnp.bfloat16), "rep", scatter_dimension=0, tiled=True
        ).astype(jnp.float32),
        lax.psum_scatter(
            bias_part.astype(jnp.bfloat16), "rep", scatter_dimension=0, tiled=True
        ).astype(jnp.float32),
    )
    piece = grad_rows
    input_sum = lax.psum_scatter(
        lax.dot_general(
            piece, w_in, (((1,), (1,)), ((), ())), preferred_element_type=jnp.float32
        ).astype(jnp.bfloat16),
        "col",
        scatter_dimension=0,
        tiled=True,
    )
    return (input_sum, w_in_sum.astype(jnp.bfloat16), bias_sum, w_out_sum.astype(jnp.bfloat16))


def solution(mesh):
    in_specs = (
        P(("col", "rep"), "row"),
        P(("col", "rep"), "row"),
        P("row", "col"),
        P("col"),
        P("col", "row"),
    )
    out_specs = (
        P(("col", "rep"), "row"),
        P("row", ("col", "rep")),
        P(("col", "rep")),
        P(("col", "rep"), "row"),
    )
    return jax.shard_map(local, mesh=mesh, in_specs=in_specs, out_specs=out_specs, check_vma=False)
```

profile of v0, /device:TPU:1, one launch (start us, length us, event | category | flops | bytes accessed | tf_op | source)
XLA Modules:
  0.0 606.4 jit_solution(7369650238327166096)
XLA Ops:
  7.2 0.0 copy-start
  7.2 0.0 all-gather.5.cloned.1.call-start
  7.2 0.7 all-gather.5.cloned.1.call-update
  7.9 0.0 all-gather.7.cloned.1.call-start
  8.0 0.7 all-gather.7.cloned.1.call-update
  8.7 0.0 reduce-scatter.6.cloned.1.call-start
  8.7 68.7 %all-gather.5.cloned.1.call-done = bf16[2048,640]{1,0:T(8,128)(2,1)} async-done(((bf16[128,640]{1,0:T(8,128)(2,1)}), bf16[2048,640]{1,0:T(8,128)(2,1)}) %all-gather.5.cloned.1.call-update) | async-done | bytes 2621456 | tf_op jit(solution)/shard_map/all_gather | solution.py:14
  77.4 6.7 %convolution_convert_fusion.1 = bf16[2048,864]{0,1:T(8,128)(2,1)} fusion(bf16[2048,640]{1,0:T(8,128)(2,1)} %all-gather.5.cloned.1.call-done, bf16[864,640]{1,0:T(8,128)(2,1)} %param.9), kind=kOutput, calls=%fused_computation.2 | convolution fusion | flops 2266693632 | bytes 7266304 | tf_op jit(solution)/shard_map/dot_general | solution.py:25
  84.1 0.0 reduce-scatter.6.cloned.1.call-update
  84.1 0.0 reduce-scatter.8.cloned.1.call-start
  84.2 65.9 %all-gather.7.cloned.1.call-done = bf16[2048,640]{1,0:T(8,128)(2,1)} async-done(((bf16[128,640]{1,0:T(8,128)(2,1)}), bf16[2048,640]{1,0:T(8,128)(2,1)}) %all-gather.7.cloned.1.call-update) | async-done | bytes 2621456 | tf_op jit(solution)/shard_map/all_gather | solution.py:13
  150.1 0.0 copy-done
  150.1 6.2 %convolution_convert_fusion = bf16[2048,864]{0,1:T(8,128)(2,1)} fusion(bf16[2048,640]{1,0:T(8,128)(2,1)} %all-gather.7.cloned.1.call-done, bf16[640,864]{0,1:T(8,128)(2,1)S(1)} %copy-done), kind=kOutput, calls=%fused_computation.1 | convolution fusion | flops 2266693632 | bytes 7266304 | tf_op jit(solution)/shard_map/dot_general | solution.py:18
  156.3 0.0 copy-start.1
  156.3 0.0 reduce-scatter.8.cloned.1.call-update
  156.3 0.0 all-gather.9.cloned.1.call-start
  156.3 90.3 %reduce-scatter.6.cloned.1.call-done = bf16[256,864]{0,1:T(8,128)(2,1)} async-done(((bf16[2048,864]{0,1:T(8,128)(2,1)}), bf16[256,864]{0,1:T(8,128)(2,1)}) %reduce-scatter.6.cloned.1.call-update) | async-done | bytes 442384 | tf_op jit(solution)/shard_map/reduce_scatter | solution.py:24
  246.7 90.2 %reduce-scatter.8.cloned.1.call-done = bf16[256,864]{0,1:T(8,128)(2,1)} async-done(((bf16[2048,864]{0,1:T(8,128)(2,1)}), bf16[256,864]{0,1:T(8,128)(2,1)}) %reduce-scatter.8.cloned.1.call-update) | async-done | bytes 442384 | tf_op jit(solution)/shard_map/reduce_scatter | solution.py:17
  336.9 0.0 copy-done.1
  336.9 2.8 multiply_convert_fusion.2
  339.7 0.0 all-gather.9.cloned.1.call-update
  339.8 0.0 all-gather.11.cloned.1.call-start
  339.8 0.5 all-gather.11.cloned.1.call-update
  340.4 0.0 reduce-scatter.12.cloned.1.call-start
  340.4 75.6 %all-gather.9.cloned.1.call-done = bf16[2048,864]{0,1:T(8,128)(2,1)} async-done(((bf16[256,864]{0,1:T(8,128)(2,1)}), bf16[2048,864]{0,1:T(8,128)(2,1)}) %all-gather.9.cloned.1.call-update) | async-done | bytes 3538960 | tf_op jit(solution)/shard_map/all_gather | solution.py:37
  416.0 6.8 %fusion = bf16[640,864]{0,1:T(8,128)(2,1)} fusion(bf16[2048,864]{0,1:T(8,128)(2,1)} %all-gather.9.cloned.1.call-done, bf16[2048,640]{1,0:T(8,128)(2,1)} %all-gather.7.cloned.1.call-done), kind=kOutput, calls=%fused_computation.6 | convolution fusion | flops 2266030080 | bytes 7266304 | tf_op jit(solution)/shard_map/dot_general | solution.py:42
  422.8 0.0 reduce-scatter.12.cloned.1.call-update
  422.8 0.0 reduce-scatter.14.cloned.1.call-start
  422.9 71.6 %all-gather.11.cloned.1.call-done = bf16[2048,864]{0,1:T(8,128)(2,1)} async-done(((bf16[256,864]{0,1:T(8,128)(2,1)}), bf16[2048,864]{0,1:T(8,128)(2,1)}) %all-gather.11.cloned.1.call-update) | async-done | bytes 3538960 | tf_op jit(solution)/shard_map/all_gather | solution.py:36
  494.5 6.7 %multiply_convert_fusion = bf16[864,640]{1,0:T(8,128)(2,1)} fusion(bf16[2048,864]{0,1:T(8,128)(2,1)} %all-gather.11.cloned.1.call-done, bf16[2048,640]{1,0:T(8,128)(2,1)} %all-gather.5.cloned.1.call-done), kind=kOutput, calls=%fused_computation.4 | convolution fusion | flops 2266030080 | bytes 7266304 | tf_op jit(solution)/shard_map/dot_general | solution.py:48
  501.2 0.0 reduce-scatter.14.cloned.1.call-update
  501.2 0.2 reduce-scatter.10.cloned.1.call-start
  501.4 6.8 %convolution_convert_fusion.2 = bf16[2048,640]{1,0:T(8,128)(2,1)} fusion(bf16[2048,864]{0,1:T(8,128)(2,1)} %all-gather.9.cloned.1.call-done, bf16[640,864]{0,1:T(8,128)(2,1)S(1)} %copy-done), kind=kOutput, calls=%fused_computation.3 | convolution fusion | flops 2266234880 | bytes 7266304 | tf_op jit(solution)/shard_map/dot_general | solution.py:67
  508.3 0.0 copy-start.2
  508.3 0.0 reduce-scatter.10.cloned.1.call-update
  508.3 0.7 copy-done.2
  509.0 0.6 dynamic-slice
  510.2 2.7 convert_reduce_fusion
  512.9 3.5 all-reduce
  516.4 0.7 dynamic-slice_convert_fusion
  517.1 0.0 reduce-scatter.12.cloned.1.call-done
  517.1 13.4 %reduce-scatter.14.cloned.1.call-done = bf16[432,640]{1,0:T(8,128)(2,1)} async-done(((bf16[864,640]{1,0:T(8,128)(2,1)}), bf16[432,640]{1,0:T(8,128)(2,1)}) %reduce-scatter.14.cloned.1.call-update) | async-done | bytes 552976 | tf_op jit(solution)/shard_map/reduce_scatter | solution.py:58
  530.5 69.4 %reduce-scatter.10.cloned.1.call-done = bf16[128,640]{1,0:T(8,128)(2,1)} async-done(((bf16[2048,640]{1,0:T(8,128)(2,1)}), bf16[128,640]{1,0:T(8,128)(2,1)}) %reduce-scatter.10.cloned.1.call-update) | async-done | bytes 163856 | tf_op jit(solution)/shard_map/reduce_scatter | solution.py:66
  (1 shorter events, 0.0 us)
Async XLA Ops:
  7.2 142.9 %copy-start = (bf16[640,864]{0,1:T(8,128)(2,1)S(1)}, bf16[640,864]{0,1:T(8,128)(2,1)}, u32[]{:S(2)}) copy-start(bf16[640,864]{0,1:T(8,128)(2,1)} %param.7) | copy-start | bytes 3317764
  7.2 70.2 %all-gather.5.cloned.1.call-start = ((), (), s32[]{:S(2)}) async-start(), calls=%async_computation.5 | async-start | bytes 2785280 | tf_op jit(solution)/shard_map/all_gather | solution.py:14
  7.9 142.2 %all-gather.7.cloned.1.call-start = ((), (), s32[]{:S(2)}) async-start(), calls=%async_computation.7 | async-start | bytes 2785280 | tf_op jit(solution)/shard_map/all_gather | solution.py:13
  8.7 238.0 %reduce-scatter.6.cloned.1.call-start = ((), (), s32[]{:S(2)}) async-start(), calls=%async_computation.6 | async-start | bytes 3981312 | tf_op jit(solution)/shard_map/reduce_scatter | solution.py:24
  84.1 252.8 %reduce-scatter.8.cloned.1.call-start = ((), (), s32[]{:S(2)}) async-start(), calls=%async_computation.8 | async-start | bytes 3981312 | tf_op jit(solution)/shard_map/reduce_scatter | solution.py:17
  156.3 180.7 %copy-start.1 = (f32[864]{0:T(1024)S(1)}, f32[864]{0:T(1024)}, u32[]{:S(2)}) copy-start(f32[864]{0:T(1024)} %param.8) | copy-start | bytes 10372
  156.3 259.7 %all-gather.9.cloned.1.call-start = ((), (), s32[]{:S(2)}) async-start(), calls=%async_computation.9 | async-start | bytes 3981312 | tf_op jit(solution)/shard_map/all_gather | solution.py:37
  339.8 154.7 %all-gather.11.cloned.1.call-start = ((), (), s32[]{:S(2)}) async-start(), calls=%async_computation.12 | async-start | bytes 3981312 | tf_op jit(solution)/shard_map/all_gather | solution.py:36
  340.4 176.7 %reduce-scatter.12.cloned.1.call-start = ((), (), s32[]{:S(2)}) async-start(), calls=%async_computation.11 | async-start | bytes 1658880 | tf_op jit(solution)/shard_map/reduce_scatter | solution.py:55
  422.8 107.7 %reduce-scatter.14.cloned.1.call-start = ((), (), s32[]{:S(2)}) async-start(), calls=%async_computation.13 | async-start | bytes 1658880 | tf_op jit(solution)/shard_map/reduce_scatter | solution.py:58
  501.2 98.7 %reduce-scatter.10.cloned.1.call-start = ((), (), s32[]{:S(2)}) async-start(), calls=%async_computation.10 | async-start | bytes 2785280 | tf_op jit(solution)/shard_map/reduce_scatter | solution.py:66
  508.3 0.7 copy-start.2
Sparse Core Ops, SparseCore 0:
  9.8 67.5 all-gather.4
  79.2 70.8 all-gather.6
  154.3 92.3 reduce-scatter.5
  251.4 85.5 reduce-scatter.7
  339.9 76.0 all-gather.8
  418.9 75.5 all-gather.10
  497.6 14.3 reduce-scatter.11
  515.2 15.2 reduce-scatter.13
  533.6 66.2 reduce-scatter.9
where the time goes:
time: 616 us; the launch traced here: 606 us
  waiting for transfers between devices  547 us (89%)
  matrix products  33.2 us (5%)
  between operations  14.5 us (2%)
  other arithmetic  6.2 us (1%)
    reduce_scatter x1, waiting for transfers between devices, local(): lax.psum_scatter(lax.dot_general(piece, w_out, (((1,), (1,)), ((), ())),...  90.3 us
    reduce_scatter x1, waiting for transfers between devices, local(): lax.psum_scatter(jnp.dot(piece, w_in, preferred_element_type=jnp.float32)...  90.2 us
    all_gather x1, waiting for transfers between devices, local(): lax.all_gather(grad_local, 'row', axis=0, tiled=True)  75.6 us
    all_gather x1, waiting for transfers between devices, local(): lax.all_gather(act_local, 'row', axis=0, tiled=True)  71.6 us
    reduce_scatter x1, waiting for transfers between devices, local(): lax.psum_scatter(lax.dot_general(piece, w_in, (((1,), (1,)), ((), ())), p...  69.4 us
    all_gather x1, waiting for transfers between devices, local(): lax.all_gather(out_grad, 'col', axis=0, tiled=True)  68.7 us
    all_gather x1, waiting for transfers between devices, local(): lax.all_gather(tokens, 'col', axis=0, tiled=True)  65.9 us
    reduce_scatter x1, waiting for transfers between devices, local(): lax.psum_scatter(w_out_part.astype(jnp.bfloat16), 'rep', scatter_dimensio...  13.4 us
  transfers between devices with their start and end apart: 9, of which 8 were waited for; matrix products, arithmetic and copies ran while one was open for 6% of the time, Pallas kernels for 0%

commit v1 on v0

v1 whole, which is shorter than its diff:
```python
import jax
import jax.numpy as jnp
from jax import lax
from jax.experimental import pallas as pl
from jax.experimental.pallas import tpu as pltpu
from jax.sharding import PartitionSpec as P

MESH = pl.DeviceIdType.MESH
BF16, F32 = jnp.bfloat16, jnp.float32
NX, NZ = 4, 8
GROUP, HALF = 128, 64
WIDTH, WIDE = 640, 1280
HID, HALF_HID = 864, 432
QUARTER, EIGHTH = 32, 16
CHUNKS = 8
SCALE = 1.0 / 64.0
ORDER = (
    [(0, slot) for slot in range(CHUNKS)]
    + [(1, slot) for slot in (0, 1, 2, 3, 7, 6, 5, 4)]
)


def contract(a, b, dim_a, dim_b):
    return lax.dot_general(
        a, b, (((dim_a,), (dim_b,)), ((), ())), preferred_element_type=F32
    )


def gelu_parts(value):
    cube = value * value * value
    bend = jnp.tanh(0.7978845608 * (value + 0.044715 * cube))
    return bend


def kernel(
    tok, og, win, bias, wout,
    ig_out, wgi_out, bg_out, wgo_out,
    xg, wi, wo, bias_v, part, first, second_out, second, ap, pre,
    ig, zr, ys, yr, wg, core_out, core_in, far_out, far_in,
    bsum, bcore, bpair, bfar,
    local_sem, send_sem, recv_sem,
):
    row, col, rep = lax.axis_index("row"), lax.axis_index("col"), lax.axis_index("rep")
    yh, x = row // NX, row % NX
    yl, z = col // NZ, col % NZ

    def at(yh_=yh, x_=x, yl_=yl, z_=z, rep_=rep):
        return {"row": yh_ * NX + x_, "col": yl_ * NZ + z_, "rep": rep_}

    x_right, x_left = at(x_=(x + 1) % NX), at(x_=(x + 3) % NX)
    z_right, z_left = at(z_=(z + 1) % NZ), at(z_=(z + 7) % NZ)
    core = at(rep_=1 - rep)
    y_far = at(yh_=1 - yh)
    y_peers = [
        (yh, 1 - yl, at(yl_=1 - yl)),
        (1 - yh, yl, y_far),
        (1 - yh, 1 - yl, at(yh_=1 - yh, yl_=1 - yl)),
    ]

    counts = {"local": 0, "remote": 0}
    sent = []

    def move(src, dst):
        copy = pltpu.make_async_copy(src, dst, local_sem.at[counts["local"]])
        counts["local"] += 1
        copy.start()
        return copy

    def send(src, dst, device):
        number = counts["remote"]
        counts["remote"] += 1
        copy = pltpu.make_async_remote_copy(
            src_ref=src,
            dst_ref=dst,
            send_sem=send_sem.at[number],
            recv_sem=recv_sem.at[number],
            device_id=device,
            device_id_type=MESH,
        )
        copy.start()
        sent.append(copy)
        return copy

    def span(start, size, unit):
        return pl.ds(pl.multiple_of(start, unit), size)

    my_rows = span(yl * HALF, HALF, HALF)
    my_lanes = span(yh * WIDTH, WIDTH, 128)
    far_lanes = span((1 - yh) * WIDTH, WIDTH, 128)

    own_x = move(tok.at[span(yh * HALF, HALF, HALF)], xg.at[0, 0, my_rows, my_lanes])
    own_g = move(og.at[span(yh * HALF, HALF, HALF)], xg.at[1, 0, my_rows, my_lanes])
    own_wi = move(win, wi.at[my_lanes])
    own_wo = move(wout, wo.at[:, my_lanes])
    own_bias = move(bias, bias_v)

    barrier = pltpu.get_barrier_semaphore()
    everyone = [x_right, x_left, z_right, z_left, core] + [p[2] for p in y_peers]
    for device in everyone:
        pl.semaphore_signal(barrier, inc=1, device_id=device, device_id_type=MESH)
    pl.semaphore_wait(barrier, len(everyone))

    def spread(j, source):
        return [
            send(
                source.at[span(to_yh * HALF, HALF, HALF)],
                xg.at[j, 0, my_rows, my_lanes],
                device,
            )
            for to_yh, _, device in y_peers
        ]

    ring = {}

    def ring_start(j):
        ring[j, 1] = [send(xg.at[j, 0], xg.at[j, 1], z_right)]
        ring[j, 2] = [send(xg.at[j, 0], xg.at[j, 2], z_left)]

    here = set()

    def arrive(j, slot):
        if slot == 0 or (j, slot) in here:
            return
        here.add((j, slot))
        for copy in ring[j, slot]:
            copy.wait_recv()

    def forward(j, slot):
        arrive(j, slot)
        device = z_right if slot % 2 else z_left
        if slot < 5:
            ring[j, slot + 2] = [send(xg.at[j, slot], xg.at[j, slot + 2], device)]
        else:
            rows = pl.ds(0 if slot == 5 else HALF, HALF)
            ring.setdefault((j, 7), []).append(
                send(xg.at[j, slot, rows], xg.at[j, 7, rows], device)
            )

    x_parts = spread(0, tok)
    half_w = span(rep * (WIDTH // 2), WIDTH // 2, 16)
    wi_mine = span(yh * WIDTH + rep * (WIDTH // 2), WIDTH // 2, 16)
    wi_theirs = span((1 - yh) * WIDTH + rep * (WIDTH // 2), WIDTH // 2, 16)
    wi_copy = send(win.at[half_w], wi.at[wi_mine], y_far)
    half_h = span(rep * HALF_HID, HALF_HID, 16)

    own_x.wait()
    for copy in x_parts:
        copy.wait_recv()
    ring_start(0)
    g_parts = spread(1, og)
    wo_copy = send(wout.at[half_h], wo.at[half_h, my_lanes], y_far)

    wi_copy.wait_recv()
    wi_core = send(wi.at[wi_theirs], wi.at[wi_theirs], core)
    forward(0, 1)
    forward(0, 2)
    own_wi.wait()
    own_bias.wait()
    wi_core.wait_recv()

    stage1, stage2, stage3, stage4 = {}, {}, {}, {}

    def quarter(of, offset=0, size=QUARTER):
        return span(((x + of) % NX) * QUARTER + offset, size, EIGHTH)

    def run1(k):
        j, slot = ORDER[k]
        arrive(j, slot)
        if j == 0:
            product = contract(xg[0, slot], wi[...], 1, 0)
        else:
            product = contract(xg[1, slot], wo[...], 1, 1)
        part[k] = product.astype(BF16)
        stage1[k] = [
            send(part.at[k, quarter(2, 0, EIGHTH)], first.at[k, 0], x_right),
            send(part.at[k, quarter(2, EIGHTH, EIGHTH)], first.at[k, 1], x_left),
        ]

    def run2(k):
        stage1[k][0].wait_recv()
        low, high = pl.ds(0, EIGHTH), pl.ds(EIGHTH, EIGHTH)
        second_out[k, 0, low] = (
            part[k, quarter(1, 0, EIGHTH)].astype(F32) + first[k, 0].astype(F32)
        ).astype(BF16)
        second_out[k, 0, high] = part[k, quarter(1, EIGHTH, EIGHTH)]
        right = send(second_out.at[k, 0], second.at[k, 0], x_right)
        stage1[k][1].wait_recv()
        second_out[k, 1, high] = (
            part[k, quarter(3, EIGHTH, EIGHTH)].astype(F32) + first[k, 1].astype(F32)
        ).astype(BF16)
        second_out[k, 1, low] = part[k, quarter(3, 0, EIGHTH)]
        left = send(second_out.at[k, 1], second.at[k, 1], x_left)
        stage2[k] = [right, left]

    def run3(k):
        j, slot = ORDER[k]
        for copy in stage2[k]:
            copy.wait_recv()
        total = (
            part[k, quarter(0)].astype(F32)
            + second[k, 0].astype(F32)
            + second[k, 1].astype(F32)
        )
        mine = quarter(0)
        if j == 0:
            value = total + bias_v[...]
            pre[slot] = value
            result = 0.5 * value * (1.0 + gelu_parts(value))
        else:
            value = pre[slot]
            bend = gelu_parts(value)
            slope = 0.7978845608 * (1.0 + 3.0 * 0.044715 * value * value)
            result = total * (
                0.5 * (1.0 + bend) + 0.5 * value * (1.0 - bend * bend) * slope
            )
        ap[j, slot, mine] = result.astype(BF16)
        block = ap.at[j, slot, mine]
        stage3[k] = [send(block, block, x_right), send(block, block, x_left)]

    def run4(k):
        j, slot = ORDER[k]
        stage3[k][0].wait_recv()
        block = ap.at[j, slot, quarter(3, 0, EIGHTH)]
        right = send(block, block, x_right)
        stage3[k][1].wait_recv()
        block = ap.at[j, slot, quarter(1, EIGHTH, EIGHTH)]
        left = send(block, block, x_left)
        stage4[k] = [right, left]

    def run5(k):
        for copy in stage4[k]:
            copy.wait_recv()

    started = set()

    def weight_grad(j, pair):
        slots = pl.ds(2 * pair, 2)
        for slot in (2 * pair, 2 * pair + 1):
            arrive(j, slot)
        left = ap[1 - j, slots].reshape(2 * GROUP, HID)
        right = xg[j, slots].reshape(2 * GROUP, WIDE)
        product = contract(left, right, 0, 0)
        if j in started:
            wg[j] += product
        else:
            started.add(j)
            wg[j] = product

    def bias_part(slot, fresh):
        rows = ap[1, slot].astype(F32).reshape(GROUP // 8, 8, HID).sum(axis=0)
        bsum[...] = rows if fresh else bsum[...] + rows

    def input_part(slot):
        ig[slot] = contract(ap[1, slot], wi[...], 1, 1).astype(BF16)

    core_copy, far_copy = {}, {}

    def core_send(j, far):
        lanes = far_lanes if far else my_lanes
        rows = span((1 - rep) * HALF_HID, HALF_HID, 16)
        core_out[j, far] = (wg[j, rows, lanes] * SCALE).astype(BF16)
        core_copy[j, far] = send(core_out.at[j, far], core_in.at[j, far], core)

    def far_send(j):
        core_copy[j, 1].wait_recv()
        rows = span(rep * HALF_HID, HALF_HID, 16)
        total = wg[j, rows, far_lanes] * SCALE + core_in[j, 1].astype(F32)
        far_out[j] = total.astype(BF16)
        far_copy[j] = send(far_out.at[j], far_in.at[j], y_far)

    def weight_final(j, out):
        core_copy[j, 0].wait_recv()
        far_copy[j].wait_recv()
        rows = span(rep * HALF_HID, HALF_HID, 16)
        total = wg[j, rows, my_lanes] * SCALE + core_in[j, 0].astype(F32)
        out[...] = (total + far_in[j].astype(F32)).astype(out.dtype)

    low, high = pl.ds(0, HALF), pl.ds(HALF, HALF)
    ring_sum = {}

    def sum_send(side, step, slot, rows, add):
        if add:
            ring_sum[side, step - 1, rows.start].wait_recv()
            ig[slot, rows] = (
                ig[slot, rows].astype(F32) + zr[side, step - 1, rows].astype(F32)
            ).astype(BF16)
        ring_sum[side, step, rows.start] = send(
            ig.at[slot, rows], zr.at[side, step, rows], z_left if side else z_right
        )

    for k in range(len(ORDER) + 4):
        if k == 1:
            forward(0, 3)
            forward(0, 4)
        if k == 3:
            forward(0, 5)
            forward(0, 6)
            own_g.wait()
            for copy in g_parts:
                copy.wait_recv()
            ring_start(1)
        if k == 4:
            wo_copy.wait_recv()
            theirs = wo.at[half_h, far_lanes]
            wo_core = send(theirs, theirs, core)
        if k == 6:
            forward(1, 1)
            forward(1, 2)
        if k == 8:
            own_wo.wait()
            wo_core.wait_recv()
            forward(1, 3)
            forward(1, 4)
        if k == 10:
            forward(1, 5)
            forward(1, 6)
        if 4 <= k:
            run5(k - 4)
        if 3 <= k < 19:
            run4(k - 3)
        if 2 <= k < 18:
            run3(k - 2)
        if 1 <= k < 17:
            run2(k - 1)
        if k < 16:
            run1(k)
        if 10 <= k < 14:
            weight_grad(1, k - 10)
        if k == 14:
            core_send(1, 1)
            core_send(1, 0)
        if k == 15:
            far_send(1)
        if k >= 12:
            slot = ORDER[k - 4][1]
            input_part(slot)
            bias_part(slot, k == 12)
        if k == 14:
            weight_grad(0, 0)
        if k == 16:
            weight_grad(0, 1)
            sum_send(0, 0, 7, low, False)
            sum_send(1, 0, 7, high, False)
        if k == 17:
            sum_send(0, 1, 6, high, False)
            sum_send(0, 1, 6, low, True)
            weight_grad(0, 3)
        if k == 18:
            sum_send(1, 1, 5, low, False)
            sum_send(1, 1, 5, high, True)
        if k == 19:
            sum_send(0, 2, 4, high, True)
            sum_send(0, 2, 4, low, True)
            weight_grad(0, 2)

    core_bias = send(bsum, bcore, core)
    core_send(0, 1)
    core_send(0, 0)
    sum_send(1, 2, 3, low, True)
    sum_send(1, 2, 3, high, True)
    far_send(0)
    core_bias.wait_recv()
    bpair[...] = bsum[...] + bcore[...]
    far_bias = send(bpair, bfar, y_far)
    sum_send(0, 3, 2, high, True)
    sum_send(0, 3, 2, low, True)
    sum_send(1, 3, 1, low, True)
    sum_send(1, 3, 1, high, True)
    weight_final(1, wgo_out)
    far_bias.wait_recv()
    total = jnp.sum(bpair[...] + bfar[...], axis=0, keepdims=True) * SCALE
    bg_out[...] = jnp.where(rep == 0, total[:, :HALF_HID], total[:, HALF_HID:])

    for rows in (low, high):
        for side in (0, 1):
            ring_sum[side, 3, rows.start].wait_recv()
        ys[rows] = (
            ig[0, rows].astype(F32)
            + zr[0, 3, rows].astype(F32)
            + zr[1, 3, rows].astype(F32)
        ).astype(BF16)
    back = [
        send(
            ys.at[span(to_yl * HALF, HALF, HALF), span(to_yh * WIDTH, WIDTH, 128)],
            yr.at[yh, yl],
            device,
        )
        for to_yh, to_yl, device in y_peers
    ]
    yr[yh, yl] = ys[my_rows, my_lanes]
    weight_final(0, wgi_out)
    for copy in back:
        copy.wait_recv()
    for half in (0, 1):
        ig_out[pl.ds(half * HALF, HALF)] = (
            yr[half, 0].astype(F32) + yr[half, 1].astype(F32)
        ).astype(BF16)
    for copy in sent:
        copy.wait_send()


def local(tokens, out_grad, w_in, bias_in, w_out):
    hbm, vmem = pl.BlockSpec(memory_space=pl.ANY), pl.BlockSpec(memory_space=pltpu.VMEM)
    steps = len(ORDER)
    ig, wgi, bg, wgo = pl.pallas_call(
        kernel,
        name="ffn_backward",
        out_shape=(
            jax.ShapeDtypeStruct((GROUP, WIDTH), BF16),
            jax.ShapeDtypeStruct((HALF_HID, WIDTH), BF16),
            jax.ShapeDtypeStruct((1, HALF_HID), F32),
            jax.ShapeDtypeStruct((HALF_HID, WIDTH), BF16),
        ),
        in_specs=[hbm] * 5,
        out_specs=(vmem,) * 4,
        scratch_shapes=[
            pltpu.VMEM((2, CHUNKS, GROUP, WIDE), BF16),
            pltpu.VMEM((WIDE, HID), BF16),
            pltpu.VMEM((HID, WIDE), BF16),
            pltpu.VMEM((1, HID), F32),
            pltpu.VMEM((steps, GROUP, HID), BF16),
            pltpu.VMEM((steps, 2, EIGHTH, HID), BF16),
            pltpu.VMEM((steps, 2, QUARTER, HID), BF16),
            pltpu.VMEM((steps, 2, QUARTER, HID), BF16),
            pltpu.VMEM((2, CHUNKS, GROUP, HID), BF16),
            pltpu.VMEM((CHUNKS, QUARTER, HID), F32),
            pltpu.VMEM((CHUNKS, GROUP, WIDE), BF16),
            pltpu.VMEM((2, 4, GROUP, WIDE), BF16),
            pltpu.VMEM((GROUP, WIDE), BF16),
            pltpu.VMEM((2, 2, HALF, WIDTH), BF16),
            pltpu.VMEM((2, HID, WIDE), F32),
            pltpu.VMEM((2, 2, HALF_HID, WIDTH), BF16),
            pltpu.VMEM((2, 2, HALF_HID, WIDTH), BF16),
            pltpu.VMEM((2, HALF_HID, WIDTH), BF16),
            pltpu.VMEM((2, HALF_HID, WIDTH), BF16),
            pltpu.VMEM((8, HID), F32),
            pltpu.VMEM((8, HID), F32),
            pltpu.VMEM((8, HID), F32),
            pltpu.VMEM((8, HID), F32),
            pltpu.SemaphoreType.DMA((5,)),
            pltpu.SemaphoreType.DMA((200,)),
            pltpu.SemaphoreType.DMA((200,)),
        ],
        compiler_params=pltpu.CompilerParams(
            collective_id=0, has_side_effects=True, vmem_limit_bytes=58 << 20
        ),
        cost_estimate=pl.CostEstimate(
            flops=11_300_000_000, bytes_accessed=4_000_000, transcendentals=0
        ),
    )(tokens, out_grad, w_in, bias_in.reshape(1, HID), w_out)
    return ig, wgi.T, bg.reshape(HALF_HID), wgo


def solution(mesh):
    in_specs = (
        P(("col", "rep"), "row"),
        P(("col", "rep"), "row"),
        P("row", "col"),
        P("col"),
        P("col", "row"),
    )
    out_specs = (
        P(("col", "rep"), "row"),
        P("row", ("col", "rep")),
        P(("col", "rep")),
        P(("col", "rep"), "row"),
    )
    return jax.shard_map(local, mesh=mesh, in_specs=in_specs, out_specs=out_specs, check_vma=False)
```

time: 616 us -> 171 us (0.28); the launches traced: 606 us -> 169 us
  waiting for transfers between devices: 547 us -> 0 us
  Pallas kernels: 0 us -> 159 us
  matrix products: 33.2 us -> 0 us
  between operations: 14.5 us -> 0.66 us
  local copies, waits for them, and re-layouts: 1.25 us -> 8.64 us
  other arithmetic: 6.2 us -> 0 us
    all_gather x4 -> x0, waiting for transfers between devices: 282 us -> none  [the longest x1 75.6 us: local(): lax.all_gather(grad_local, 'row', axis=0, tiled=True)]
    reduce_scatter x5 -> x0, waiting for transfers between devices: 263 us -> none  [the longest x1 90.3 us: local(): lax.psum_scatter(lax.dot_general(piece, w_out, (((1,), (1,)), ((), ())),...]
    pallas_call x0 -> x1, Pallas kernels: none -> 159 us  [local(): pl.pallas_call(kernel, name='ffn_backward', out_shape=(jax.ShapeDtypeStru...]
    dot_general x5 -> x0, matrix products: 33.2 us -> none  [the longest x1 6.83 us: local(): lax.dot_general(piece, w_in, (((1,), (1,)), ((), ())), preferred_element_...]
  transfers between devices with their start and end apart: 9 -> 0, of which waited for: 8 -> 0; matrix products, arithmetic and copies ran while one was open for 6% -> 0% of each run, Pallas kernels for 0% -> 0%
where the time goes in v1:
time: 171 us; the launch traced here: 169 us
  Pallas kernels  159 us (93%)
  local copies, waits for them, and re-layouts  8.64 us (5%)
    pallas_call x1, Pallas kernels, local(): pl.pallas_call(kernel, name='ffn_backward', out_shape=(jax.ShapeDtypeStru...  159 us
    unnamed x9, local copies, waits for them, and re-layouts  7.37 us

profile of v1, /device:TPU:1, one launch (start us, length us, event | category | flops | bytes accessed | tf_op | source)
XLA Modules:
  0.0 168.7 jit_solution(16808923867589271750)
XLA Ops:
  0.6 1.3 reshape.14.bias
  1.9 2.4 %copy.9.win = bf16[640,864]{1,0:T(8,128)(2,1)} copy(bf16[640,864]{0,1:T(8,128)(2,1)} %param.7) | data formatting | bytes 2211840 | tf_op args[2]
  4.3 159.4 %ffn_backward.1 = (bf16[128,640]{1,0:T(8,128)(2,1)}, bf16[432,640]{1,0:T(8,128)(2,1)}, f32[1,432]{1,0:T(1,128)}, bf16[432,640]{1,0:T(8,128)(2,1)}) custom-call(bf16[128,640]{1,0:T(8,128)(2,1)} %tok.1, bf16[128,640]{1,0:T(8,128)(2,1)} %og.1, bf16[640,864]{1,0:T(8,128)(2,1)} %copy.9.win, f32[1,864]{1,0:T(1,128)} %reshape.14.bias, bf16[864,640]{1,0:T(8,128)(2,1)} %wout.1), custom_call_target="tpu_custom_call" | custom-call | flops 11299999744 | bytes 4000000 | tf_op jit(solution)/shard_map/ffn_backward/pallas_call | solution.py:405
  163.8 0.0 copy-start.1
  163.8 0.0 copy-start
  163.8 1.7 copy.14
  165.4 1.9 %copy.15 = bf16[640,432]{0,1:T(8,128)(2,1)} copy(bf16[640,432]{0,1:T(8,128)(2,1)} %bitcast.2) | data formatting | bytes 1105920
  167.3 0.0 copy-done.1
  167.3 0.6 copy.16
  167.9 0.0 copy-done
  167.9 0.8 copy.17
Async XLA Ops:
  163.8 3.6 %copy-start.1 = (f32[1,432]{1,0:T(1,128)S(1)}, f32[1,432]{1,0:T(1,128)}, u32[]{:S(2)}) copy-start(f32[1,432]{1,0:T(1,128)} %get-tuple-element.10) | copy-start | bytes 5188
  163.8 4.2 %copy-start = (bf16[432,640]{1,0:T(8,128)(2,1)S(1)}, bf16[432,640]{1,0:T(8,128)(2,1)}, u32[]{:S(2)}) copy-start(bf16[432,640]{1,0:T(8,128)(2,1)} %get-tuple-element.19) | copy-start | bytes 1658884

commit v2 on v0

v2 whole, which is shorter than its diff:
```python
import jax
import jax.numpy as jnp
from jax import lax
from jax.experimental import pallas as pl
from jax.experimental.pallas import tpu as pltpu
from jax.sharding import PartitionSpec as P

MESH = pl.DeviceIdType.MESH
BF16, F32 = jnp.bfloat16, jnp.float32
NX, NZ = 4, 8
GROUP, HALF = 128, 64
WIDTH, WIDE = 640, 1280
HID, CORE_HID = 864, 432
PADDED = 896
PARTS = ((0, 192), (192, 240))
PLACE = (0, 384)
LANES = ((0, 384), (384, 512), (0, 896))
QUARTER, EIGHTH = 32, 16
CHUNKS = 8
SCALE = 1.0 / 64.0
SCHEDULE = (
    ("sx",), ("zs", 0), ("wf", 0, 0), ("zf", 0, 1, 0), ("zf", 0, 2, 1), ("r1", 0, 0, 0), ("zf", 0, 1, 1),
    ("r1", 0, 0, 1), ("zf", 0, 2, 0), ("r1", 0, 0, 2), ("r2", 0, 0, 0), ("wf", 0, 1), ("r2", 0, 0, 1),
    ("zf", 0, 3, 0), ("zf", 0, 4, 1), ("r2", 0, 0, 2), ("r3", 0, 0, 0), ("r1", 0, 1, 0), ("r3", 0, 0, 1),
    ("r1", 0, 1, 1), ("r3", 0, 0, 2), ("zf", 0, 4, 0), ("r4", 0, 0, 0), ("r1", 0, 1, 4), ("zf", 0, 3, 1),
    ("r1", 0, 0, 3), ("r2", 0, 1, 0), ("r1", 0, 0, 4), ("r2", 0, 1, 1), ("r4", 0, 0, 1), ("r4", 0, 0, 2),
    ("r5", 0, 0, 0), ("r1", 0, 1, 3), ("zf", 0, 6, 1), ("zf", 0, 5, 0), ("wf", 1, 0), ("zs", 1),
    ("r3", 0, 1, 0), ("r2", 0, 1, 4), ("r2", 0, 0, 4), ("r2", 0, 0, 3), ("r3", 0, 1, 1), ("r5", 0, 0, 1),
    ("r5", 0, 0, 2), ("r2", 0, 1, 3), ("r4", 0, 1, 0), ("r1", 0, 0, 6), ("r3", 0, 1, 4), ("r3", 0, 0, 4),
    ("r3", 0, 0, 3), ("r4", 0, 1, 1), ("wf", 1, 1), ("r1", 0, 0, 5), ("r3", 0, 1, 3), ("r2", 0, 0, 6),
    ("r5", 0, 1, 0), ("r4", 0, 1, 4), ("r1", 0, 0, 7), ("r4", 0, 0, 4), ("r1", 0, 1, 5), ("zf", 1, 2, 1),
    ("zf", 1, 1, 0), ("r2", 0, 0, 5), ("r1", 0, 1, 6), ("r4", 0, 1, 3), ("r1", 0, 1, 2), ("r5", 0, 1, 4),
    ("r3", 0, 0, 6), ("r2", 0, 0, 7), ("r5", 0, 0, 4), ("r5", 0, 1, 1), ("r4", 0, 0, 3), ("r2", 0, 1, 5),
    ("zf", 1, 1, 1), ("zf", 1, 2, 0), ("wg", 1, 2, 0), ("r3", 0, 0, 5), ("r5", 0, 1, 3), ("r2", 0, 1, 2),
    ("r4", 0, 0, 6), ("r2", 0, 1, 6), ("r3", 0, 0, 7), ("r5", 0, 0, 3), ("zf", 1, 3, 0), ("zf", 1, 4, 1),
    ("r3", 0, 1, 5), ("r4", 0, 0, 5), ("r1", 0, 1, 7), ("r3", 0, 1, 2), ("r5", 0, 0, 6), ("r1", 1, 0, 2),
    ("r1", 1, 0, 1), ("r4", 0, 0, 7), ("zf", 1, 4, 0), ("zf", 1, 3, 1), ("r1", 1, 0, 3), ("r5", 0, 0, 5),
    ("r4", 0, 1, 5), ("r1", 1, 0, 4), ("r2", 0, 1, 7), ("r1", 1, 1, 4), ("r4", 0, 1, 2), ("r2", 1, 0, 1),
    ("r2", 1, 0, 2), ("r5", 0, 0, 7), ("r3", 0, 1, 6), ("zf", 1, 6, 1), ("r2", 1, 0, 3), ("zf", 1, 5, 0),
    ("r5", 0, 1, 5), ("r2", 1, 0, 4), ("r3", 0, 1, 7), ("r2", 1, 1, 4), ("r5", 0, 1, 2), ("wg", 1, 2, 1),
    ("r3", 1, 0, 2), ("r3", 1, 0, 1), ("r4", 0, 1, 6), ("wg", 1, 2, 2), ("r3", 1, 0, 4), ("r4", 0, 1, 7),
    ("r3", 1, 0, 3), ("r3", 1, 1, 4), ("r4", 1, 0, 2), ("r1", 1, 0, 5), ("r1", 1, 0, 6), ("r1", 1, 0, 7),
    ("r4", 1, 0, 4), ("r1", 1, 1, 7), ("r4", 1, 0, 3), ("r1", 1, 1, 6), ("r5", 1, 0, 2), ("r1", 1, 1, 5),
    ("r2", 1, 0, 5), ("r2", 1, 0, 6), ("r2", 1, 0, 7), ("r5", 1, 0, 4), ("r4", 1, 1, 4), ("r4", 1, 0, 1),
    ("r2", 1, 1, 7), ("r5", 1, 0, 3), ("r5", 0, 1, 7), ("r5", 0, 1, 6), ("wg", 1, 2, 3), ("r2", 1, 1, 5),
    ("r3", 1, 0, 5), ("r2", 1, 1, 6), ("r3", 1, 0, 6), ("cs", 1, 1), ("r3", 1, 0, 7), ("r5", 1, 1, 4),
    ("ip", 4), ("r5", 1, 0, 1), ("wg", 0, 0, 1), ("r3", 1, 1, 7), ("cs", 1, 0), ("r1", 1, 0, 0),
    ("r4", 1, 0, 5), ("r1", 1, 1, 2), ("r3", 1, 1, 6), ("fs", 1, 1), ("r4", 1, 0, 6), ("r1", 1, 1, 3),
    ("fs", 1, 0), ("r4", 1, 0, 7), ("r4", 1, 1, 7), ("r3", 1, 1, 5), ("r2", 1, 0, 0), ("r5", 1, 0, 5),
    ("wg", 0, 0, 2), ("r1", 1, 1, 1), ("r1", 1, 1, 0), ("r2", 1, 1, 3), ("r5", 1, 0, 7), ("r4", 1, 1, 6),
    ("r5", 1, 1, 7), ("ip", 7), ("ss", 1, 0, 1), ("r4", 1, 1, 5), ("ss", 0, 0, 0), ("r2", 1, 1, 2),
    ("r3", 1, 0, 0), ("r2", 1, 1, 1), ("bp", 7), ("r5", 1, 0, 6), ("r2", 1, 1, 0), ("wg", 0, 0, 3),
    ("r3", 1, 1, 3), ("r5", 1, 1, 6), ("ip", 6), ("ss", 0, 1, 1), ("bp", 6), ("r5", 1, 1, 5), ("ip", 5),
    ("ss", 1, 1, 0), ("r4", 1, 0, 0), ("r3", 1, 1, 2), ("wg", 0, 1, 2), ("r3", 1, 1, 1), ("ss", 1, 1, 1),
    ("ss", 0, 1, 0), ("r3", 1, 1, 0), ("r4", 1, 1, 3), ("r5", 1, 0, 0), ("wg", 0, 0, 0), ("r4", 1, 1, 2),
    ("cs", 0, 0), ("bp", 5), ("wg", 0, 1, 3), ("r4", 1, 1, 1), ("wo", 1, 0), ("r4", 1, 1, 0),
    ("ss", 0, 2, 1), ("r5", 1, 1, 3), ("ip", 3), ("ss", 1, 2, 0), ("fs", 0, 0), ("r5", 1, 1, 2), ("ip", 2),
    ("r5", 1, 1, 1), ("ip", 1), ("r5", 1, 1, 0), ("ip", 0), ("wg", 0, 1, 0), ("ss", 1, 2, 1),
    ("ss", 0, 2, 0), ("wg", 0, 1, 1), ("cs", 0, 1), ("bp", 3), ("bp", 0), ("bp", 1), ("wo", 1, 1), ("bp", 2),
    ("bp", 4), ("bc",), ("ss", 0, 3, 1), ("ss", 1, 3, 0), ("fs", 0, 1), ("wo", 0, 0), ("bf",),
    ("ss", 0, 3, 0), ("ss", 1, 3, 1), ("wo", 0, 1), ("yb",), ("bo",), ("io",),
)


def contract(a, b, dim_a, dim_b):
    return lax.dot_general(
        a, b, (((dim_a,), (dim_b,)), ((), ())), preferred_element_type=F32
    )


def bend_of(value):
    return jnp.tanh(0.7978845608 * (value + 0.044715 * value * value * value))


def kernel(
    tok, og, win, bias, wout,
    ig_out, wgi_out, bg_out, wgo_out,
    xg, wi, wo, bias_raw, bias_v, part, first, second_out, second, ap, pre,
    ig, zr, ys, yr, wg, core_out, core_in, far_out, far_in,
    bsum, bcore, bpair, bfar,
    local_sem, send_sem, recv_sem,
):
    row, col, rep = lax.axis_index("row"), lax.axis_index("col"), lax.axis_index("rep")
    yh, x = row // NX, row % NX
    yl, z = col // NZ, col % NZ

    def at(yh_=yh, x_=x, yl_=yl, z_=z, rep_=rep):
        return {"row": yh_ * NX + x_, "col": yl_ * NZ + z_, "rep": rep_}

    x_right, x_left = at(x_=(x + 1) % NX), at(x_=(x + 3) % NX)
    z_right, z_left = at(z_=(z + 1) % NZ), at(z_=(z + 7) % NZ)
    core = at(rep_=1 - rep)
    y_far = at(yh_=1 - yh)
    y_peers = [
        (yh, 1 - yl, at(yl_=1 - yl)),
        (1 - yh, yl, y_far),
        (1 - yh, 1 - yl, at(yh_=1 - yh, yl_=1 - yl)),
    ]

    counts = {"local": 0, "remote": 0}
    sent, arrived = [], set()

    def move(src, dst):
        copy = pltpu.make_async_copy(src, dst, local_sem.at[counts["local"]])
        counts["local"] += 1
        copy.start()
        return copy

    def send(src, dst, device):
        number = counts["remote"]
        counts["remote"] += 1
        copy = pltpu.make_async_remote_copy(
            src_ref=src,
            dst_ref=dst,
            send_sem=send_sem.at[number],
            recv_sem=recv_sem.at[number],
            device_id=device,
            device_id_type=MESH,
        )
        copy.start()
        sent.append(copy)
        return copy

    def need(*copies):
        for copy in copies:
            if id(copy) not in arrived:
                arrived.add(id(copy))
                copy.wait_recv()

    def span(start, size, unit):
        return pl.ds(pl.multiple_of(start, unit), size)

    my_rows = span(yl * HALF, HALF, HALF)
    my_lanes = span(yh * WIDTH, WIDTH, 128)
    far_lanes = span((1 - yh) * WIDTH, WIDTH, 128)

    def source_rows(which, of):
        start, size = PARTS[of]
        return span(which * CORE_HID + start, size, 16)

    def held_rows(which, of):
        size = PARTS[of][1]
        return span(PLACE[of] + which * size, size, 16)

    own = {}
    for j, (block, weights, held) in enumerate(((tok, win, wi), (og, wout, wo))):
        own[j] = [
            move(block.at[span(yh * HALF, HALF, HALF)], xg.at[j, 0, my_rows, my_lanes])
        ]
        for of in (0, 1):
            own[j, of] = [
                move(
                    weights.at[pl.ds(which * CORE_HID + PARTS[of][0], PARTS[of][1])],
                    held.at[
                        pl.ds(PLACE[of] + which * PARTS[of][1], PARTS[of][1]), my_lanes
                    ],
                )
                for which in (0, 1)
            ]
    own_bias = [move(bias, bias_raw)]

    def own_ready(key):
        while own[key]:
            own[key].pop().wait()

    own["bias"] = own_bias

    def bias_ready():
        if not own["bias"]:
            return
        own_ready("bias")
        raw = bias_raw[...].reshape(1, HID)
        blocks = [
            raw[:, which * CORE_HID + start : which * CORE_HID + start + size]
            for start, size in PARTS
            for which in (0, 1)
        ]
        blocks.append(jnp.zeros((1, PADDED - HID), F32))
        bias_v[...] = jnp.concatenate(blocks, axis=1)

    for held in (wi, wo):
        held[pl.ds(HID, PADDED - HID)] = jnp.zeros((PADDED - HID, WIDE), BF16)

    barrier = pltpu.get_barrier_semaphore()
    everyone = [x_right, x_left, z_right, z_left, core] + [p[2] for p in y_peers]
    for device in everyone:
        pl.semaphore_signal(barrier, inc=1, device_id=device, device_id_type=MESH)
    pl.semaphore_wait(barrier, len(everyone))

    spread, weight_far, weight_core, ring = {}, {}, {}, {}
    halves = (pl.ds(0, HALF), pl.ds(HALF, HALF))

    def send_block(j):
        source = og if j else tok
        spread[j] = [
            send(
                source.at[span(to_yh * HALF, HALF, HALF)],
                xg.at[j, 0, my_rows, my_lanes],
                device,
            )
            for to_yh, _, device in y_peers
        ]

    def send_weights(j, of):
        source, held = (wout, wo) if j else (win, wi)
        weight_far[j, of] = send(
            source.at[source_rows(rep, of)], held.at[held_rows(rep, of), my_lanes], y_far
        )

    def begin():
        send_block(0)
        send_weights(0, 0)

    def ring_send(j, source, slot, half, device):
        rows = halves[half]
        ring[j, slot, half] = send(xg.at[j, source, rows], xg.at[j, slot, rows], device)

    def ring_start(j):
        own_ready(j)
        need(*spread[j])
        for half in (0, 1):
            ring_send(j, 0, 1, half, z_right)
            ring_send(j, 0, 2, 1 - half, z_left)
        if j == 0:
            send_weights(0, 1)

    def ring_pass(j, slot, half):
        need(ring[j, slot, half])
        ring_send(j, slot, min(slot + 2, 7), half, z_right if slot % 2 else z_left)

    def chunk_ready(j, slot):
        if slot == 0:
            own_ready(j)
            need(*spread[j])
        else:
            need(ring[j, slot, 0], ring[j, slot, 1])

    def weights_pass(j, of):
        need(weight_far[j, of])
        block = (wo if j else wi).at[held_rows(rep, of), far_lanes]
        weight_core[j, of] = send(block, block, core)
        if (j, of) == (0, 0):
            send_block(1)
        if (j, of) == (0, 1):
            send_weights(1, 0)
            send_weights(1, 1)

    def weights_ready(j, lanes):
        for of in (0, 1):
            if lanes in (of, 2):
                own_ready((j, of))
                need(weight_core[j, of])

    stage = {}

    def quarter(of, offset=0, size=QUARTER):
        return span(((x + of) % NX) * QUARTER + offset, size, EIGHTH)

    low16, high16 = pl.ds(0, EIGHTH), pl.ds(EIGHTH, EIGHTH)

    def multiply(j, lanes, slot):
        chunk_ready(j, slot)
        weights_ready(j, lanes)
        at_lanes = pl.ds(*LANES[lanes])
        weights = (wo if j else wi)[at_lanes]
        part[j, slot, :, at_lanes] = contract(xg[j, slot], weights, 1, 1).astype(BF16)
        rows = (quarter(2, 0, EIGHTH), quarter(2, EIGHTH, EIGHTH))
        stage[1, j, lanes, slot] = [
            send(
                part.at[j, slot, rows[side], at_lanes],
                first.at[j, slot, side, :, at_lanes],
                x_left if side else x_right,
            )
            for side in (0, 1)
        ]

    def add_first(j, lanes, slot):
        at_lanes = pl.ds(*LANES[lanes])
        copies = []
        for side in (0, 1):
            need(stage[1, j, lanes, slot][side])
            of = 3 if side else 1
            summed = (high16, EIGHTH) if side else (low16, 0)
            plain = (low16, 0) if side else (high16, EIGHTH)
            second_out[j, slot, side, summed[0], at_lanes] = (
                part[j, slot, quarter(of, summed[1], EIGHTH), at_lanes].astype(F32)
                + first[j, slot, side, :, at_lanes].astype(F32)
            ).astype(BF16)
            second_out[j, slot, side, plain[0], at_lanes] = part[
                j, slot, quarter(of, plain[1], EIGHTH), at_lanes
            ]
            copies.append(
                send(
                    second_out.at[j, slot, side, :, at_lanes],
                    second.at[j, slot, side, :, at_lanes],
                    x_left if side else x_right,
                )
            )
        stage[2, j, lanes, slot] = copies

    def activate(j, lanes, slot):
        need(*stage[2, j, lanes, slot])
        at_lanes = pl.ds(*LANES[lanes])
        mine = quarter(0)
        total = (
            part[j, slot, mine, at_lanes].astype(F32)
            + second[j, slot, 0, :, at_lanes].astype(F32)
            + second[j, slot, 1, :, at_lanes].astype(F32)
        )
        if j == 0:
            bias_ready()
            value = total + bias_v[:, at_lanes]
            pre[slot, :, at_lanes] = value
            result = 0.5 * value * (1.0 + bend_of(value))
        else:
            value = pre[slot, :, at_lanes]
            bend = bend_of(value)
            slope = 0.7978845608 * (1.0 + 3.0 * 0.044715 * value * value)
            result = total * (
                0.5 * (1.0 + bend) + 0.5 * value * (1.0 - bend * bend) * slope
            )
        ap[j, slot, mine, at_lanes] = result.astype(BF16)
        block = ap.at[j, slot, mine, at_lanes]
        stage[3, j, lanes, slot] = [send(block, block, x_right), send(block, block, x_left)]

    def hand_on(j, lanes, slot):
        at_lanes = pl.ds(*LANES[lanes])
        copies = []
        for side in (0, 1):
            need(stage[3, j, lanes, slot][side])
            rows = quarter(1, EIGHTH, EIGHTH) if side else quarter(3, 0, EIGHTH)
            block = ap.at[j, slot, rows, at_lanes]
            copies.append(send(block, block, x_left if side else x_right))
        stage[4, j, lanes, slot] = copies

    def all_here(j, lanes, slot):
        need(*stage[4, j, lanes, slot])

    core_copy, far_copy = {}, {}
    started = set()

    def weight_grad(j, lanes, pair):
        for slot in (2 * pair, 2 * pair + 1):
            chunk_ready(j, slot)
        slots, hidden = pl.ds(2 * pair, 2), pl.ds(*LANES[lanes])
        left = ap[1 - j, slots, :, hidden].reshape(2 * GROUP, LANES[lanes][1])
        right = xg[j, slots].reshape(2 * GROUP, WIDE)
        product = contract(left, right, 0, 0)
        wg[j, hidden] = wg[j, hidden] + product if (j, lanes) in started else product
        started.add((j, lanes))

    def core_send(j, of):
        rows = pl.ds(*PARTS[of])
        for far, lanes in ((1, far_lanes), (0, my_lanes)):
            block = wg[j, held_rows(1 - rep, of), lanes] * SCALE
            core_out[j, far, rows] = block.astype(BF16)
            core_copy[j, of, far] = send(
                core_out.at[j, far, rows], core_in.at[j, far, rows], core
            )

    def far_send(j, of):
        need(core_copy[j, of, 1])
        rows = pl.ds(*PARTS[of])
        block = wg[j, held_rows(rep, of), far_lanes] * SCALE
        far_out[j, rows] = (block + core_in[j, 1, rows].astype(F32)).astype(BF16)
        far_copy[j, of] = send(far_out.at[j, rows], far_in.at[j, rows], y_far)

    def weight_out(j, of):
        need(core_copy[j, of, 0], far_copy[j, of])
        rows = pl.ds(*PARTS[of])
        block = wg[j, held_rows(rep, of), my_lanes] * SCALE
        total = block + core_in[j, 0, rows].astype(F32)
        out = wgo_out if j else wgi_out
        out[rows] = (total + far_in[j, rows].astype(F32)).astype(BF16)

    bias_copy = {}

    def bias_part(slot):
        rows = ap[1, slot].astype(F32).reshape(GROUP // 8, 8, PADDED).sum(axis=0)
        bsum[...] = bsum[...] + rows if "bias" in started else rows
        started.add("bias")

    def bias_core():
        bias_copy[0] = send(bsum, bcore, core)

    def bias_far():
        need(bias_copy[0])
        bpair[...] = bsum[...] + bcore[...]
        bias_copy[1] = send(bpair, bfar, y_far)

    def bias_out():
        need(bias_copy[1])
        total = jnp.sum(bpair[...] + bfar[...], axis=0, keepdims=True) * SCALE
        mine = [
            jnp.concatenate(
                [
                    total[:, PLACE[of] + which * size : PLACE[of] + (which + 1) * size]
                    for of, (_, size) in enumerate(PARTS)
                ],
                axis=1,
            )
            for which in (0, 1)
        ]
        bg_out[...] = jnp.where(rep == 0, mine[0], mine[1])

    ring_sum, back = {}, []

    def input_part(slot):
        ig[slot] = contract(ap[1, slot], wi[...], 1, 0).astype(BF16)

    def sum_pass(side, step, half):
        slot = ((7, 6, 4, 2), (7, 5, 3, 1))[side][step]
        rows = halves[half]
        if (side, step - 1, half) in ring_sum:
            need(ring_sum[side, step - 1, half])
            ig[slot, rows] = (
                ig[slot, rows].astype(F32) + zr[side, step - 1, rows].astype(F32)
            ).astype(BF16)
        ring_sum[side, step, half] = send(
            ig.at[slot, rows], zr.at[side, step, rows], z_left if side else z_right
        )

    def sum_end():
        for half, rows in enumerate(halves):
            need(ring_sum[0, 3, half], ring_sum[1, 3, half])
            ys[rows] = (
                ig[0, rows].astype(F32)
                + zr[0, 3, rows].astype(F32)
                + zr[1, 3, rows].astype(F32)
            ).astype(BF16)
        for to_yh, to_yl, device in y_peers:
            lanes = span(to_yh * WIDTH, WIDTH, 128)
            block = ys.at[span(to_yl * HALF, HALF, HALF), lanes]
            back.append(send(block, yr.at[yh, yl], device))
        yr[yh, yl] = ys[my_rows, my_lanes]

    def input_out():
        need(*back)
        for half, rows in enumerate(halves):
            total = yr[half, 0].astype(F32) + yr[half, 1].astype(F32)
            ig_out[rows] = total.astype(BF16)

    steps = {
        "sx": begin, "zs": ring_start, "zf": ring_pass, "wf": weights_pass,
        "r1": multiply, "r2": add_first, "r3": activate, "r4": hand_on, "r5": all_here,
        "wg": weight_grad, "cs": core_send, "fs": far_send, "wo": weight_out,
        "bp": bias_part, "bc": bias_core, "bf": bias_far, "bo": bias_out,
        "ip": input_part, "ss": sum_pass, "yb": sum_end, "io": input_out,
    }
    for name, *which in SCHEDULE:
        steps[name](*which)
    for copy in sent:
        copy.wait_send()


def hand_over(*refs):
    for source, target in zip(refs[:4], refs[4:]):
        target[...] = source[...]


def local(tokens, out_grad, w_in, bias_in, w_out):
    hbm, vmem = pl.BlockSpec(memory_space=pl.ANY), pl.BlockSpec(memory_space=pltpu.VMEM)
    ig, wgi, bg, wgo = pl.pallas_call(
        kernel,
        name="ffn_backward",
        out_shape=(
            jax.ShapeDtypeStruct((GROUP, WIDTH), BF16),
            jax.ShapeDtypeStruct((CORE_HID, WIDTH), BF16),
            jax.ShapeDtypeStruct((1, CORE_HID), F32),
            jax.ShapeDtypeStruct((CORE_HID, WIDTH), BF16),
        ),
        in_specs=[hbm] * 5,
        out_specs=(vmem,) * 4,
        scratch_shapes=[
            pltpu.VMEM((2, CHUNKS, GROUP, WIDE), BF16),
            pltpu.VMEM((PADDED, WIDE), BF16),
            pltpu.VMEM((PADDED, WIDE), BF16),
            pltpu.VMEM((HID,), F32),
            pltpu.VMEM((1, PADDED), F32),
            pltpu.VMEM((2, CHUNKS, GROUP, PADDED), BF16),
            pltpu.VMEM((2, CHUNKS, 2, EIGHTH, PADDED), BF16),
            pltpu.VMEM((2, CHUNKS, 2, QUARTER, PADDED), BF16),
            pltpu.VMEM((2, CHUNKS, 2, QUARTER, PADDED), BF16),
            pltpu.VMEM((2, CHUNKS, GROUP, PADDED), BF16),
            pltpu.VMEM((CHUNKS, QUARTER, PADDED), F32),
            pltpu.VMEM((CHUNKS, GROUP, WIDE), BF16),
            pltpu.VMEM((2, 4, GROUP, WIDE), BF16),
            pltpu.VMEM((GROUP, WIDE), BF16),
            pltpu.VMEM((2, 2, HALF, WIDTH), BF16),
            pltpu.VMEM((2, PADDED, WIDE), F32),
            pltpu.VMEM((2, 2, CORE_HID, WIDTH), BF16),
            pltpu.VMEM((2, 2, CORE_HID, WIDTH), BF16),
            pltpu.VMEM((2, CORE_HID, WIDTH), BF16),
            pltpu.VMEM((2, CORE_HID, WIDTH), BF16),
            pltpu.VMEM((8, PADDED), F32),
            pltpu.VMEM((8, PADDED), F32),
            pltpu.VMEM((8, PADDED), F32),
            pltpu.VMEM((8, PADDED), F32),
            pltpu.SemaphoreType.DMA((11,)),
            pltpu.SemaphoreType.DMA((360,)),
            pltpu.SemaphoreType.DMA((360,)),
        ],
        compiler_params=pltpu.CompilerParams(
            collective_id=0, has_side_effects=True, vmem_limit_bytes=58 << 20
        ),
        cost_estimate=pl.CostEstimate(
            flops=11_300_000_000, bytes_accessed=4_000_000, transcendentals=0
        ),
    )(tokens, out_grad, w_in.T, bias_in, w_out)
    ig, wgi, bg, wgo = pl.pallas_call(
        hand_over,
        name="hand_over",
        out_shape=tuple(jax.ShapeDtypeStruct(v.shape, v.dtype) for v in (ig, wgi, bg, wgo)),
        in_specs=[vmem] * 4,
        out_specs=(vmem,) * 4,
    )(ig, wgi, bg, wgo)
    return ig, wgi.T, bg.reshape(CORE_HID), wgo


def solution(mesh):
    in_specs = (
        P(("col", "rep"), "row"),
        P(("col", "rep"), "row"),
        P("row", "col"),
        P("col"),
        P("col", "row"),
    )
    out_specs = (
        P(("col", "rep"), "row"),
        P("row", ("col", "rep")),
        P(("col", "rep")),
        P(("col", "rep"), "row"),
    )
    return jax.shard_map(local, mesh=mesh, in_specs=in_specs, out_specs=out_specs, check_vma=False)
```

time: 616 us -> 135 us (0.22); the launches traced: 606 us -> 134 us
  waiting for transfers between devices: 547 us -> 0 us
  Pallas kernels: 0 us -> 134 us
  matrix products: 33.2 us -> 0 us
  between operations: 14.5 us -> 0.64 us
  other arithmetic: 6.2 us -> 0 us
    all_gather x4 -> x0, waiting for transfers between devices: 282 us -> none  [the longest x1 75.6 us: local(): lax.all_gather(grad_local, 'row', axis=0, tiled=True)]
    reduce_scatter x5 -> x0, waiting for transfers between devices: 263 us -> none  [the longest x1 90.3 us: local(): lax.psum_scatter(lax.dot_general(piece, w_out, (((1,), (1,)), ((), ())),...]
    pallas_call x0 -> x2, Pallas kernels: none -> 134 us  [the longest x1 131 us: local(): pl.pallas_call(kernel, name='ffn_backward', out_shape=(jax.ShapeDtypeStru...]
    dot_general x5 -> x0, matrix products: 33.2 us -> none  [the longest x1 6.83 us: local(): lax.dot_general(piece, w_in, (((1,), (1,)), ((), ())), preferred_element_...]
  transfers between devices with their start and end apart: 9 -> 0, of which waited for: 8 -> 0; matrix products, arithmetic and copies ran while one was open for 6% -> 0% of each run, Pallas kernels for 0% -> 0%
where the time goes in v2:
time: 135 us; the launch traced here: 134 us
  Pallas kernels  134 us (99%)
    pallas_call x1, Pallas kernels, local(): pl.pallas_call(kernel, name='ffn_backward', out_shape=(jax.ShapeDtypeStru...  131 us

profile of v2, /device:TPU:1, one launch (start us, length us, event | category | flops | bytes accessed | tf_op | source)
XLA Modules:
  0.0 134.3 jit_solution(4395046288978899187)
XLA Ops:
  0.6 131.2 %ffn_backward.1 = (bf16[128,640]{1,0:T(8,128)(2,1)}, bf16[432,640]{1,0:T(8,128)(2,1)}, f32[1,432]{1,0:T(1,128)}, bf16[432,640]{1,0:T(8,128)(2,1)}) custom-call(bf16[128,640]{1,0:T(8,128)(2,1)} %tok.1, bf16[128,640]{1,0:T(8,128)(2,1)} %og.1, bf16[864,640]{1,0:T(8,128)(2,1)} %bitcast.3, f32[864]{0:T(1024)} %bias.1, bf16[864,640]{1,0:T(8,128)(2,1)} %wout.1), custom_call_target="tpu_custom_call" | custom-call | flops 11299999744 | bytes 4000000 | tf_op jit(solution)/shard_map/ffn_backward/pallas_call | solution.py:463
  131.9 2.4 %hand_over.1 = (bf16[128,640]{1,0:T(8,128)(2,1)}, bf16[432,640]{1,0:T(8,128)(2,1)}, f32[1,432]{1,0:T(1,128)}, bf16[432,640]{1,0:T(8,128)(2,1)}) custom-call(bf16[128,640]{1,0:T(8,128)(2,1)} %get-tuple-element.12.refs_0_, bf16[432,640]{1,0:T(8,128)(2,1)} %get-tuple-element.13.refs_1_, f32[1,432]{1,0:T(1,128)} %get-tuple-element.14.refs_2_, ...), custom_call_target="tpu_custom_call" | custom-call | tf_op jit(solution)/shard_map/hand_over/pallas_call | solution.py:510

commit v3 on v2

--- a/solution.py
+++ b/solution.py
@@ -18,47 +18,48 @@
 QUARTER, EIGHTH = 32, 16
 CHUNKS = 8
 SCALE = 1.0 / 64.0
+DIRECT = ((1, 0, 7), (1, 1, 7))
 SCHEDULE = (
     ("sx",), ("zs", 0), ("wf", 0, 0), ("zf", 0, 1, 0), ("zf", 0, 2, 1), ("r1", 0, 0, 0), ("zf", 0, 1, 1),
-    ("r1", 0, 0, 1), ("zf", 0, 2, 0), ("r1", 0, 0, 2), ("r2", 0, 0, 0), ("wf", 0, 1), ("r2", 0, 0, 1),
-    ("zf", 0, 3, 0), ("zf", 0, 4, 1), ("r2", 0, 0, 2), ("r3", 0, 0, 0), ("r1", 0, 1, 0), ("r3", 0, 0, 1),
-    ("r1", 0, 1, 1), ("r3", 0, 0, 2), ("zf", 0, 4, 0), ("r4", 0, 0, 0), ("r1", 0, 1, 4), ("zf", 0, 3, 1),
-    ("r1", 0, 0, 3), ("r2", 0, 1, 0), ("r1", 0, 0, 4), ("r2", 0, 1, 1), ("r4", 0, 0, 1), ("r4", 0, 0, 2),
-    ("r5", 0, 0, 0), ("r1", 0, 1, 3), ("zf", 0, 6, 1), ("zf", 0, 5, 0), ("wf", 1, 0), ("zs", 1),
-    ("r3", 0, 1, 0), ("r2", 0, 1, 4), ("r2", 0, 0, 4), ("r2", 0, 0, 3), ("r3", 0, 1, 1), ("r5", 0, 0, 1),
-    ("r5", 0, 0, 2), ("r2", 0, 1, 3), ("r4", 0, 1, 0), ("r1", 0, 0, 6), ("r3", 0, 1, 4), ("r3", 0, 0, 4),
-    ("r3", 0, 0, 3), ("r4", 0, 1, 1), ("wf", 1, 1), ("r1", 0, 0, 5), ("r3", 0, 1, 3), ("r2", 0, 0, 6),
-    ("r5", 0, 1, 0), ("r4", 0, 1, 4), ("r1", 0, 0, 7), ("r4", 0, 0, 4), ("r1", 0, 1, 5), ("zf", 1, 2, 1),
-    ("zf", 1, 1, 0), ("r2", 0, 0, 5), ("r1", 0, 1, 6), ("r4", 0, 1, 3), ("r1", 0, 1, 2), ("r5", 0, 1, 4),
-    ("r3", 0, 0, 6), ("r2", 0, 0, 7), ("r5", 0, 0, 4), ("r5", 0, 1, 1), ("r4", 0, 0, 3), ("r2", 0, 1, 5),
-    ("zf", 1, 1, 1), ("zf", 1, 2, 0), ("wg", 1, 2, 0), ("r3", 0, 0, 5), ("r5", 0, 1, 3), ("r2", 0, 1, 2),
-    ("r4", 0, 0, 6), ("r2", 0, 1, 6), ("r3", 0, 0, 7), ("r5", 0, 0, 3), ("zf", 1, 3, 0), ("zf", 1, 4, 1),
-    ("r3", 0, 1, 5), ("r4", 0, 0, 5), ("r1", 0, 1, 7), ("r3", 0, 1, 2), ("r5", 0, 0, 6), ("r1", 1, 0, 2),
-    ("r1", 1, 0, 1), ("r4", 0, 0, 7), ("zf", 1, 4, 0), ("zf", 1, 3, 1), ("r1", 1, 0, 3), ("r5", 0, 0, 5),
-    ("r4", 0, 1, 5), ("r1", 1, 0, 4), ("r2", 0, 1, 7), ("r1", 1, 1, 4), ("r4", 0, 1, 2), ("r2", 1, 0, 1),
-    ("r2", 1, 0, 2), ("r5", 0, 0, 7), ("r3", 0, 1, 6), ("zf", 1, 6, 1), ("r2", 1, 0, 3), ("zf", 1, 5, 0),
-    ("r5", 0, 1, 5), ("r2", 1, 0, 4), ("r3", 0, 1, 7), ("r2", 1, 1, 4), ("r5", 0, 1, 2), ("wg", 1, 2, 1),
-    ("r3", 1, 0, 2), ("r3", 1, 0, 1), ("r4", 0, 1, 6), ("wg", 1, 2, 2), ("r3", 1, 0, 4), ("r4", 0, 1, 7),
-    ("r3", 1, 0, 3), ("r3", 1, 1, 4), ("r4", 1, 0, 2), ("r1", 1, 0, 5), ("r1", 1, 0, 6), ("r1", 1, 0, 7),
-    ("r4", 1, 0, 4), ("r1", 1, 1, 7), ("r4", 1, 0, 3), ("r1", 1, 1, 6), ("r5", 1, 0, 2), ("r1", 1, 1, 5),
-    ("r2", 1, 0, 5), ("r2", 1, 0, 6), ("r2", 1, 0, 7), ("r5", 1, 0, 4), ("r4", 1, 1, 4), ("r4", 1, 0, 1),
-    ("r2", 1, 1, 7), ("r5", 1, 0, 3), ("r5", 0, 1, 7), ("r5", 0, 1, 6), ("wg", 1, 2, 3), ("r2", 1, 1, 5),
-    ("r3", 1, 0, 5), ("r2", 1, 1, 6), ("r3", 1, 0, 6), ("cs", 1, 1), ("r3", 1, 0, 7), ("r5", 1, 1, 4),
-    ("ip", 4), ("r5", 1, 0, 1), ("wg", 0, 0, 1), ("r3", 1, 1, 7), ("cs", 1, 0), ("r1", 1, 0, 0),
-    ("r4", 1, 0, 5), ("r1", 1, 1, 2), ("r3", 1, 1, 6), ("fs", 1, 1), ("r4", 1, 0, 6), ("r1", 1, 1, 3),
-    ("fs", 1, 0), ("r4", 1, 0, 7), ("r4", 1, 1, 7), ("r3", 1, 1, 5), ("r2", 1, 0, 0), ("r5", 1, 0, 5),
-    ("wg", 0, 0, 2), ("r1", 1, 1, 1), ("r1", 1, 1, 0), ("r2", 1, 1, 3), ("r5", 1, 0, 7), ("r4", 1, 1, 6),
-    ("r5", 1, 1, 7), ("ip", 7), ("ss", 1, 0, 1), ("r4", 1, 1, 5), ("ss", 0, 0, 0), ("r2", 1, 1, 2),
-    ("r3", 1, 0, 0), ("r2", 1, 1, 1), ("bp", 7), ("r5", 1, 0, 6), ("r2", 1, 1, 0), ("wg", 0, 0, 3),
-    ("r3", 1, 1, 3), ("r5", 1, 1, 6), ("ip", 6), ("ss", 0, 1, 1), ("bp", 6), ("r5", 1, 1, 5), ("ip", 5),
-    ("ss", 1, 1, 0), ("r4", 1, 0, 0), ("r3", 1, 1, 2), ("wg", 0, 1, 2), ("r3", 1, 1, 1), ("ss", 1, 1, 1),
-    ("ss", 0, 1, 0), ("r3", 1, 1, 0), ("r4", 1, 1, 3), ("r5", 1, 0, 0), ("wg", 0, 0, 0), ("r4", 1, 1, 2),
-    ("cs", 0, 0), ("bp", 5), ("wg", 0, 1, 3), ("r4", 1, 1, 1), ("wo", 1, 0), ("r4", 1, 1, 0),
-    ("ss", 0, 2, 1), ("r5", 1, 1, 3), ("ip", 3), ("ss", 1, 2, 0), ("fs", 0, 0), ("r5", 1, 1, 2), ("ip", 2),
-    ("r5", 1, 1, 1), ("ip", 1), ("r5", 1, 1, 0), ("ip", 0), ("wg", 0, 1, 0), ("ss", 1, 2, 1),
-    ("ss", 0, 2, 0), ("wg", 0, 1, 1), ("cs", 0, 1), ("bp", 3), ("bp", 0), ("bp", 1), ("wo", 1, 1), ("bp", 2),
-    ("bp", 4), ("bc",), ("ss", 0, 3, 1), ("ss", 1, 3, 0), ("fs", 0, 1), ("wo", 0, 0), ("bf",),
-    ("ss", 0, 3, 0), ("ss", 1, 3, 1), ("wo", 0, 1), ("yb",), ("bo",), ("io",),
+    ("zf", 0, 2, 0), ("r1", 0, 0, 1), ("r1", 0, 0, 2), ("wf", 0, 1), ("r2", 0, 0, 0), ("zf", 0, 3, 0),
+    ("zf", 0, 4, 1), ("r2", 0, 0, 1), ("r2", 0, 0, 2), ("r1", 0, 1, 0), ("r3", 0, 0, 0), ("r1", 0, 1, 1),
+    ("r1", 0, 1, 2), ("zf", 0, 3, 1), ("r1", 0, 0, 4), ("zf", 0, 4, 0), ("r3", 0, 0, 1), ("r1", 0, 1, 3),
+    ("r2", 0, 1, 0), ("r1", 0, 0, 3), ("r4", 0, 0, 0), ("r1", 0, 1, 4), ("wf", 1, 0), ("zf", 0, 5, 0),
+    ("r2", 0, 1, 2), ("r2", 0, 0, 4), ("zf", 0, 6, 1), ("zs", 1), ("r4", 0, 0, 1), ("r2", 0, 1, 3),
+    ("r3", 0, 0, 2), ("r2", 0, 1, 1), ("r3", 0, 1, 0), ("r2", 0, 0, 3), ("r5", 0, 0, 0), ("r2", 0, 1, 4),
+    ("r3", 0, 1, 2), ("r3", 0, 0, 4), ("r5", 0, 0, 1), ("r3", 0, 1, 3), ("r4", 0, 0, 2), ("wf", 1, 1),
+    ("r3", 0, 1, 1), ("r4", 0, 1, 0), ("r1", 0, 0, 7), ("r1", 0, 1, 7), ("r1", 1, 0, 0), ("r3", 0, 1, 4),
+    ("r1", 0, 0, 6), ("r4", 0, 0, 4), ("zf", 1, 1, 0), ("zf", 1, 2, 1), ("r1", 0, 1, 6), ("r1", 0, 1, 5),
+    ("r4", 0, 1, 1), ("r4", 0, 1, 2), ("r1", 0, 0, 5), ("r2", 0, 0, 7), ("r4", 0, 1, 3), ("r2", 0, 1, 7),
+    ("r2", 1, 0, 0), ("r3", 0, 0, 3), ("zf", 1, 1, 1), ("r5", 0, 1, 0), ("r5", 0, 0, 2), ("r4", 0, 1, 4),
+    ("zf", 1, 2, 0), ("r2", 0, 0, 6), ("r5", 0, 0, 4), ("r2", 0, 1, 6), ("r2", 0, 1, 5), ("r5", 0, 1, 1),
+    ("wg", 1, 2, 0), ("zf", 1, 3, 0), ("r2", 0, 0, 5), ("zf", 1, 4, 1), ("r3", 0, 0, 7), ("r5", 0, 1, 3),
+    ("r5", 0, 1, 2), ("r3", 0, 1, 7), ("r3", 1, 0, 0), ("r4", 0, 0, 3), ("r5", 0, 1, 4), ("r1", 1, 0, 1),
+    ("zf", 1, 3, 1), ("r3", 0, 0, 6), ("r3", 0, 1, 6), ("zf", 1, 4, 0), ("r3", 0, 1, 5), ("r3", 0, 0, 5),
+    ("r4", 0, 0, 7), ("r1", 1, 0, 4), ("r4", 0, 1, 7), ("r1", 1, 0, 2), ("r4", 1, 0, 0), ("zf", 1, 5, 0),
+    ("r2", 1, 0, 1), ("zf", 1, 6, 1), ("r5", 0, 0, 3), ("wg", 1, 2, 1), ("r4", 0, 0, 6), ("r4", 0, 1, 6),
+    ("r4", 0, 1, 5), ("r1", 1, 1, 4), ("r4", 0, 0, 5), ("r5", 0, 0, 7), ("r1", 1, 0, 3), ("r1", 1, 1, 6),
+    ("r5", 1, 0, 0), ("r2", 1, 0, 4), ("r1", 1, 0, 6), ("r3", 1, 0, 1), ("r5", 0, 0, 6), ("r1", 1, 1, 5),
+    ("r1", 1, 0, 5), ("r2", 1, 1, 4), ("r5", 0, 1, 7), ("r1", 1, 0, 7), ("r1", 1, 1, 7), ("r2", 1, 1, 6),
+    ("r3", 1, 0, 4), ("r5", 0, 0, 5), ("r2", 1, 0, 6), ("r5", 0, 1, 6), ("r4", 1, 0, 1), ("wg", 1, 2, 3),
+    ("r3", 1, 1, 4), ("r2", 1, 1, 5), ("r2", 1, 0, 5), ("r5", 0, 1, 5), ("wg", 1, 2, 2), ("cs", 1, 1),
+    ("r1", 1, 1, 3), ("r3", 1, 1, 7), ("r3", 1, 1, 6), ("r3", 1, 0, 7), ("r4", 1, 0, 4), ("r2", 1, 0, 3),
+    ("r2", 1, 0, 2), ("r3", 1, 0, 6), ("r5", 1, 0, 1), ("cs", 1, 0), ("wg", 0, 0, 0), ("fs", 1, 1),
+    ("r4", 1, 1, 4), ("r3", 1, 1, 5), ("r3", 1, 0, 5), ("r2", 1, 1, 3), ("fs", 1, 0), ("r5", 1, 1, 7),
+    ("r4", 1, 1, 6), ("r5", 1, 0, 7), ("ip", 7), ("ss", 0, 0, 0), ("r5", 1, 0, 4), ("ss", 1, 0, 1),
+    ("r3", 1, 0, 3), ("r1", 1, 1, 0), ("r1", 1, 1, 1), ("r4", 1, 0, 6), ("r5", 1, 1, 4), ("ip", 4),
+    ("r4", 1, 1, 5), ("r1", 1, 1, 2), ("r4", 1, 0, 5), ("bp", 7), ("r3", 1, 0, 2), ("r3", 1, 1, 3),
+    ("wo", 1, 1), ("r5", 1, 1, 6), ("wg", 0, 1, 3), ("r2", 1, 1, 0), ("r4", 1, 0, 3), ("r2", 1, 1, 1),
+    ("r5", 1, 0, 6), ("ip", 6), ("r5", 1, 1, 5), ("ss", 0, 1, 1), ("r2", 1, 1, 2), ("ss", 0, 1, 0),
+    ("r5", 1, 0, 5), ("ip", 5), ("r4", 1, 0, 2), ("ss", 1, 1, 0), ("ss", 1, 1, 1), ("r4", 1, 1, 3),
+    ("bp", 5), ("wg", 0, 1, 2), ("r3", 1, 1, 0), ("r5", 1, 0, 3), ("wo", 1, 0), ("wg", 0, 0, 3),
+    ("r3", 1, 1, 2), ("bp", 6), ("r3", 1, 1, 1), ("wg", 0, 0, 2), ("r5", 1, 1, 3), ("ip", 3), ("bp", 4),
+    ("bp", 3), ("ss", 0, 2, 1), ("r4", 1, 1, 0), ("r5", 1, 0, 2), ("wg", 0, 0, 1), ("cs", 0, 0),
+    ("ss", 1, 2, 0), ("r4", 1, 1, 2), ("r4", 1, 1, 1), ("r5", 1, 1, 0), ("ss", 0, 2, 0), ("ip", 0),
+    ("bp", 0), ("fs", 0, 0), ("r5", 1, 1, 2), ("ss", 1, 2, 1), ("ip", 2), ("r5", 1, 1, 1), ("ip", 1),
+    ("bp", 2), ("wg", 0, 1, 0), ("ss", 0, 3, 1), ("bp", 1), ("bc",), ("wg", 0, 1, 1), ("cs", 0, 1),
+    ("ss", 1, 3, 0), ("ss", 0, 3, 0), ("bf",), ("ss", 1, 3, 1), ("fs", 0, 1), ("wo", 0, 0), ("bo",), ("yb",),
+    ("wo", 0, 1), ("io",),
 )
 
 
@@ -75,7 +76,7 @@
 def kernel(
     tok, og, win, bias, wout,
     ig_out, wgi_out, bg_out, wgo_out,
-    xg, wi, wo, bias_raw, bias_v, part, first, second_out, second, ap, pre,
+    xg, wi, wo, bias_raw, bias_v, part, first, second_out, second, across, ap, pre,
     ig, zr, ys, yr, wg, core_out, core_in, far_out, far_in,
     bsum, bcore, bpair, bfar,
     local_sem, send_sem, recv_sem,
@@ -88,6 +89,7 @@
         return {"row": yh_ * NX + x_, "col": yl_ * NZ + z_, "rep": rep_}
 
     x_right, x_left = at(x_=(x + 1) % NX), at(x_=(x + 3) % NX)
+    x_across = at(x_=(x + 2) % NX)
     z_right, z_left = at(z_=(z + 1) % NZ), at(z_=(z + 7) % NZ)
     core = at(rep_=1 - rep)
     y_far = at(yh_=1 - yh)
@@ -182,7 +184,7 @@
         held[pl.ds(HID, PADDED - HID)] = jnp.zeros((PADDED - HID, WIDE), BF16)
 
     barrier = pltpu.get_barrier_semaphore()
-    everyone = [x_right, x_left, z_right, z_left, core] + [p[2] for p in y_peers]
+    everyone = [x_right, x_left, x_across, z_right, z_left, core] + [p[2] for p in y_peers]
     for device in everyone:
         pl.semaphore_signal(barrier, inc=1, device_id=device, device_id_type=MESH)
     pl.semaphore_wait(barrier, len(everyone))
@@ -264,6 +266,16 @@
         at_lanes = pl.ds(*LANES[lanes])
         weights = (wo if j else wi)[at_lanes]
         part[j, slot, :, at_lanes] = contract(xg[j, slot], weights, 1, 1).astype(BF16)
+        if (j, lanes, slot) in DIRECT:
+            stage[2, j, lanes, slot] = [
+                send(part.at[j, slot, quarter(of), at_lanes], target, device)
+                for of, target, device in (
+                    (2, across.at[j, slot, :, at_lanes], x_across),
+                    (1, second.at[j, slot, 0, :, at_lanes], x_right),
+                    (3, second.at[j, slot, 1, :, at_lanes], x_left),
+                )
+            ]
+            return
         rows = (quarter(2, 0, EIGHTH), quarter(2, EIGHTH, EIGHTH))
         stage[1, j, lanes, slot] = [
             send(
@@ -307,6 +319,9 @@
             + second[j, slot, 0, :, at_lanes].astype(F32)
             + second[j, slot, 1, :, at_lanes].astype(F32)
         )
+        direct = (j, lanes, slot) in DIRECT
+        if direct:
+            total = total + across[j, slot, :, at_lanes].astype(F32)
         if j == 0:
             bias_ready()
             value = total + bias_v[:, at_lanes]
@@ -321,7 +336,10 @@
             )
         ap[j, slot, mine, at_lanes] = result.astype(BF16)
         block = ap.at[j, slot, mine, at_lanes]
-        stage[3, j, lanes, slot] = [send(block, block, x_right), send(block, block, x_left)]
+        others = [x_across] * direct + [x_right, x_left]
+        stage[4 if direct else 3, j, lanes, slot] = [
+            send(block, block, device) for device in others
+        ]
 
     def hand_on(j, lanes, slot):
         at_lanes = pl.ds(*LANES[lanes])
@@ -454,8 +472,13 @@
 
 
 def hand_over(*refs):
-    for source, target in zip(refs[:4], refs[4:]):
-        target[...] = source[...]
+    copies = [
+        pltpu.make_async_copy(refs[n], refs[4 + n], refs[8].at[n]) for n in range(4)
+    ]
+    for copy in copies:
+        copy.start()
+    for copy in copies:
+        copy.wait()
 
 
 def local(tokens, out_grad, w_in, bias_in, w_out):
@@ -464,10 +487,10 @@
         kernel,
         name="ffn_backward",
         out_shape=(
-            jax.ShapeDtypeStruct((GROUP, WIDTH), BF16),
-            jax.ShapeDtypeStruct((CORE_HID, WIDTH), BF16),
-            jax.ShapeDtypeStruct((1, CORE_HID), F32),
-            jax.ShapeDtypeStruct((CORE_HID, WIDTH), BF16),
+            pltpu.VMEM((GROUP, WIDTH), BF16),
+            pltpu.VMEM((CORE_HID, WIDTH), BF16),
+            pltpu.VMEM((1, CORE_HID), F32),
+            pltpu.VMEM((CORE_HID, WIDTH), BF16),
         ),
         in_specs=[hbm] * 5,
         out_specs=(vmem,) * 4,
@@ -481,6 +504,7 @@
             pltpu.VMEM((2, CHUNKS, 2, EIGHTH, PADDED), BF16),
             pltpu.VMEM((2, CHUNKS, 2, QUARTER, PADDED), BF16),
             pltpu.VMEM((2, CHUNKS, 2, QUARTER, PADDED), BF16),
+            pltpu.VMEM((2, CHUNKS, QUARTER, PADDED), BF16),
             pltpu.VMEM((2, CHUNKS, GROUP, PADDED), BF16),
             pltpu.VMEM((CHUNKS, QUARTER, PADDED), F32),
             pltpu.VMEM((CHUNKS, GROUP, WIDE), BF16),
@@ -512,8 +536,9 @@
         name="hand_over",
         out_shape=tuple(jax.ShapeDtypeStruct(v.shape, v.dtype) for v in (ig, wgi, bg, wgo)),
         in_specs=[vmem] * 4,
-        out_specs=(vmem,) * 4,
-    )(ig, wgi, bg, wgo)
+        out_specs=(hbm,) * 4,
+        scratch_shapes=[pltpu.SemaphoreType.DMA((4,))],
+    )(*(pltpu.with_memory_space_constraint(v, pltpu.VMEM) for v in (ig, wgi, bg, wgo)))
     return ig, wgi.T, bg.reshape(CORE_HID), wgo
 
 

time: 135 us -> 128 us (0.948)
  Pallas kernels: 134 us -> 127 us
    pallas_call x1, Pallas kernels: 131 us -> 126 us  [local(): pl.pallas_call(kernel, name='ffn_backward', out_shape=(pltpu.VMEM((GROUP,...]
where the time goes in v3:
time: 128 us
  Pallas kernels  127 us (99%)
    pallas_call x1, Pallas kernels, local(): pl.pallas_call(kernel, name='ffn_backward', out_shape=(pltpu.VMEM((GROUP,...  126 us

profile of v3, /device:TPU:1, one launch (start us, length us, event | category | flops | bytes accessed | tf_op | source)
XLA Modules:
  0.0 128.2 jit_solution(17125377147543015398)
XLA Ops:
  0.6 126.3 %ffn_backward.1 = (bf16[128,640]{1,0:T(8,128)(2,1)S(1)}, bf16[432,640]{1,0:T(8,128)(2,1)S(1)}, f32[1,432]{1,0:T(1,128)S(1)}, bf16[432,640]{1,0:T(8,128)(2,1)S(1)}) custom-call(bf16[128,640]{1,0:T(8,128)(2,1)} %tok.1, bf16[128,640]{1,0:T(8,128)(2,1)} %og.1, bf16[864,640]{1,0:T(8,128)(2,1)} %bitcast.3, f32[864]{0:T(1024)} %bias.1, bf16[864,640]{1,0:T(8,128)(2,1)} %wout.1), custom_call_target="tpu_custom_call" | custom-call | flops 11299999744 | bytes 4000000 | tf_op jit(solution)/shard_map/ffn_backward/pallas_call | solution.py:486
  127.0 1.1 hand_over.1

commit v4 on v3

--- a/solution.py
+++ b/solution.py
@@ -20,46 +20,48 @@
 SCALE = 1.0 / 64.0
 DIRECT = ((1, 0, 7), (1, 1, 7))
 SCHEDULE = (
-    ("sx",), ("zs", 0), ("wf", 0, 0), ("zf", 0, 1, 0), ("zf", 0, 2, 1), ("r1", 0, 0, 0), ("zf", 0, 1, 1),
-    ("zf", 0, 2, 0), ("r1", 0, 0, 1), ("r1", 0, 0, 2), ("wf", 0, 1), ("r2", 0, 0, 0), ("zf", 0, 3, 0),
-    ("zf", 0, 4, 1), ("r2", 0, 0, 1), ("r2", 0, 0, 2), ("r1", 0, 1, 0), ("r3", 0, 0, 0), ("r1", 0, 1, 1),
-    ("r1", 0, 1, 2), ("zf", 0, 3, 1), ("r1", 0, 0, 4), ("zf", 0, 4, 0), ("r3", 0, 0, 1), ("r1", 0, 1, 3),
-    ("r2", 0, 1, 0), ("r1", 0, 0, 3), ("r4", 0, 0, 0), ("r1", 0, 1, 4), ("wf", 1, 0), ("zf", 0, 5, 0),
-    ("r2", 0, 1, 2), ("r2", 0, 0, 4), ("zf", 0, 6, 1), ("zs", 1), ("r4", 0, 0, 1), ("r2", 0, 1, 3),
-    ("r3", 0, 0, 2), ("r2", 0, 1, 1), ("r3", 0, 1, 0), ("r2", 0, 0, 3), ("r5", 0, 0, 0), ("r2", 0, 1, 4),
-    ("r3", 0, 1, 2), ("r3", 0, 0, 4), ("r5", 0, 0, 1), ("r3", 0, 1, 3), ("r4", 0, 0, 2), ("wf", 1, 1),
-    ("r3", 0, 1, 1), ("r4", 0, 1, 0), ("r1", 0, 0, 7), ("r1", 0, 1, 7), ("r1", 1, 0, 0), ("r3", 0, 1, 4),
-    ("r1", 0, 0, 6), ("r4", 0, 0, 4), ("zf", 1, 1, 0), ("zf", 1, 2, 1), ("r1", 0, 1, 6), ("r1", 0, 1, 5),
-    ("r4", 0, 1, 1), ("r4", 0, 1, 2), ("r1", 0, 0, 5), ("r2", 0, 0, 7), ("r4", 0, 1, 3), ("r2", 0, 1, 7),
-    ("r2", 1, 0, 0), ("r3", 0, 0, 3), ("zf", 1, 1, 1), ("r5", 0, 1, 0), ("r5", 0, 0, 2), ("r4", 0, 1, 4),
-    ("zf", 1, 2, 0), ("r2", 0, 0, 6), ("r5", 0, 0, 4), ("r2", 0, 1, 6), ("r2", 0, 1, 5), ("r5", 0, 1, 1),
-    ("wg", 1, 2, 0), ("zf", 1, 3, 0), ("r2", 0, 0, 5), ("zf", 1, 4, 1), ("r3", 0, 0, 7), ("r5", 0, 1, 3),
-    ("r5", 0, 1, 2), ("r3", 0, 1, 7), ("r3", 1, 0, 0), ("r4", 0, 0, 3), ("r5", 0, 1, 4), ("r1", 1, 0, 1),
-    ("zf", 1, 3, 1), ("r3", 0, 0, 6), ("r3", 0, 1, 6), ("zf", 1, 4, 0), ("r3", 0, 1, 5), ("r3", 0, 0, 5),
-    ("r4", 0, 0, 7), ("r1", 1, 0, 4), ("r4", 0, 1, 7), ("r1", 1, 0, 2), ("r4", 1, 0, 0), ("zf", 1, 5, 0),
-    ("r2", 1, 0, 1), ("zf", 1, 6, 1), ("r5", 0, 0, 3), ("wg", 1, 2, 1), ("r4", 0, 0, 6), ("r4", 0, 1, 6),
-    ("r4", 0, 1, 5), ("r1", 1, 1, 4), ("r4", 0, 0, 5), ("r5", 0, 0, 7), ("r1", 1, 0, 3), ("r1", 1, 1, 6),
-    ("r5", 1, 0, 0), ("r2", 1, 0, 4), ("r1", 1, 0, 6), ("r3", 1, 0, 1), ("r5", 0, 0, 6), ("r1", 1, 1, 5),
-    ("r1", 1, 0, 5), ("r2", 1, 1, 4), ("r5", 0, 1, 7), ("r1", 1, 0, 7), ("r1", 1, 1, 7), ("r2", 1, 1, 6),
-    ("r3", 1, 0, 4), ("r5", 0, 0, 5), ("r2", 1, 0, 6), ("r5", 0, 1, 6), ("r4", 1, 0, 1), ("wg", 1, 2, 3),
-    ("r3", 1, 1, 4), ("r2", 1, 1, 5), ("r2", 1, 0, 5), ("r5", 0, 1, 5), ("wg", 1, 2, 2), ("cs", 1, 1),
-    ("r1", 1, 1, 3), ("r3", 1, 1, 7), ("r3", 1, 1, 6), ("r3", 1, 0, 7), ("r4", 1, 0, 4), ("r2", 1, 0, 3),
-    ("r2", 1, 0, 2), ("r3", 1, 0, 6), ("r5", 1, 0, 1), ("cs", 1, 0), ("wg", 0, 0, 0), ("fs", 1, 1),
-    ("r4", 1, 1, 4), ("r3", 1, 1, 5), ("r3", 1, 0, 5), ("r2", 1, 1, 3), ("fs", 1, 0), ("r5", 1, 1, 7),
-    ("r4", 1, 1, 6), ("r5", 1, 0, 7), ("ip", 7), ("ss", 0, 0, 0), ("r5", 1, 0, 4), ("ss", 1, 0, 1),
-    ("r3", 1, 0, 3), ("r1", 1, 1, 0), ("r1", 1, 1, 1), ("r4", 1, 0, 6), ("r5", 1, 1, 4), ("ip", 4),
-    ("r4", 1, 1, 5), ("r1", 1, 1, 2), ("r4", 1, 0, 5), ("bp", 7), ("r3", 1, 0, 2), ("r3", 1, 1, 3),
-    ("wo", 1, 1), ("r5", 1, 1, 6), ("wg", 0, 1, 3), ("r2", 1, 1, 0), ("r4", 1, 0, 3), ("r2", 1, 1, 1),
-    ("r5", 1, 0, 6), ("ip", 6), ("r5", 1, 1, 5), ("ss", 0, 1, 1), ("r2", 1, 1, 2), ("ss", 0, 1, 0),
-    ("r5", 1, 0, 5), ("ip", 5), ("r4", 1, 0, 2), ("ss", 1, 1, 0), ("ss", 1, 1, 1), ("r4", 1, 1, 3),
-    ("bp", 5), ("wg", 0, 1, 2), ("r3", 1, 1, 0), ("r5", 1, 0, 3), ("wo", 1, 0), ("wg", 0, 0, 3),
-    ("r3", 1, 1, 2), ("bp", 6), ("r3", 1, 1, 1), ("wg", 0, 0, 2), ("r5", 1, 1, 3), ("ip", 3), ("bp", 4),
-    ("bp", 3), ("ss", 0, 2, 1), ("r4", 1, 1, 0), ("r5", 1, 0, 2), ("wg", 0, 0, 1), ("cs", 0, 0),
-    ("ss", 1, 2, 0), ("r4", 1, 1, 2), ("r4", 1, 1, 1), ("r5", 1, 1, 0), ("ss", 0, 2, 0), ("ip", 0),
-    ("bp", 0), ("fs", 0, 0), ("r5", 1, 1, 2), ("ss", 1, 2, 1), ("ip", 2), ("r5", 1, 1, 1), ("ip", 1),
-    ("bp", 2), ("wg", 0, 1, 0), ("ss", 0, 3, 1), ("bp", 1), ("bc",), ("wg", 0, 1, 1), ("cs", 0, 1),
-    ("ss", 1, 3, 0), ("ss", 0, 3, 0), ("bf",), ("ss", 1, 3, 1), ("fs", 0, 1), ("wo", 0, 0), ("bo",), ("yb",),
-    ("wo", 0, 1), ("io",),
+    ("sx",), ("zs", 0), ("wf", 0, 0), ("zf", 0, 1, 0), ("zf", 0, 2, 1), ("r1", 0, 0, 0), ("r1", 0, 0, 1),
+    ("zf", 0, 2, 0), ("zf", 0, 1, 1), ("r1", 0, 0, 2), ("r2", 0, 0, 0), ("wf", 0, 1), ("zf", 0, 3, 0),
+    ("zf", 0, 4, 1), ("r2", 0, 0, 1), ("r2", 0, 0, 2), ("r1", 0, 1, 0), ("r3", 0, 0, 0), ("ra", 0, 0, 0),
+    ("r1", 0, 1, 1), ("r1", 0, 1, 2), ("r1", 0, 0, 3), ("r3", 0, 0, 1), ("ra", 0, 0, 1), ("zf", 0, 4, 0),
+    ("zf", 0, 3, 1), ("r3", 0, 0, 2), ("ra", 0, 0, 2), ("r1", 0, 1, 3), ("r2", 0, 1, 0), ("r4", 0, 0, 0),
+    ("r1", 0, 0, 4), ("r2", 0, 1, 1), ("r2", 0, 1, 2), ("zf", 0, 5, 0), ("zf", 0, 6, 1), ("r2", 0, 0, 3),
+    ("zs", 1), ("r4", 0, 0, 1), ("wf", 1, 0), ("r4", 0, 0, 2), ("r1", 0, 1, 4), ("r2", 0, 1, 3),
+    ("r3", 0, 1, 0), ("ra", 0, 1, 0), ("r5", 0, 0, 0), ("r2", 0, 0, 4), ("r1", 0, 1, 5), ("r1", 1, 0, 0),
+    ("r1", 0, 0, 6), ("r3", 0, 0, 3), ("r5", 0, 0, 1), ("ra", 0, 0, 3), ("r1", 0, 0, 5), ("r5", 0, 0, 2),
+    ("r2", 0, 1, 4), ("r1", 0, 1, 6), ("wf", 1, 1), ("r1", 0, 0, 7), ("r4", 0, 1, 0), ("r1", 0, 1, 7),
+    ("r3", 0, 0, 4), ("r2", 0, 1, 5), ("ra", 0, 0, 4), ("r2", 1, 0, 0), ("r2", 0, 0, 6), ("r3", 0, 1, 3),
+    ("r3", 0, 1, 2), ("r3", 0, 1, 1), ("r4", 0, 0, 3), ("r2", 0, 0, 5), ("zf", 1, 1, 0), ("zf", 1, 2, 1),
+    ("r3", 0, 1, 4), ("ra", 0, 1, 3), ("r2", 0, 1, 6), ("r2", 0, 0, 7), ("r5", 0, 1, 0), ("r2", 0, 1, 7),
+    ("r3", 0, 1, 5), ("r4", 0, 0, 4), ("zf", 1, 1, 1), ("zf", 1, 2, 0), ("r3", 1, 0, 0), ("r3", 0, 0, 6),
+    ("ra", 0, 0, 6), ("r5", 0, 0, 3), ("ra", 0, 1, 1), ("r3", 0, 0, 5), ("ra", 0, 0, 5), ("r4", 0, 1, 3),
+    ("r1", 1, 0, 1), ("zf", 1, 4, 1), ("r3", 0, 1, 6), ("ra", 0, 1, 6), ("zf", 1, 3, 0), ("r3", 0, 0, 7),
+    ("ra", 0, 0, 7), ("r3", 0, 1, 7), ("ra", 0, 1, 2), ("r5", 0, 0, 4), ("r4", 1, 0, 0), ("ra", 0, 1, 4),
+    ("r4", 0, 0, 6), ("r4", 0, 1, 1), ("zf", 1, 3, 1), ("zf", 1, 4, 0), ("r1", 1, 0, 4), ("r5", 0, 1, 3),
+    ("r1", 1, 0, 3), ("r2", 1, 0, 1), ("r1", 1, 1, 4), ("ra", 0, 1, 5), ("r4", 0, 0, 7), ("r4", 0, 1, 6),
+    ("r4", 0, 0, 5), ("r4", 0, 1, 2), ("r5", 1, 0, 0), ("zf", 1, 5, 0), ("zf", 1, 6, 1), ("ra", 0, 1, 7),
+    ("r4", 0, 1, 4), ("r5", 0, 0, 6), ("r5", 0, 1, 1), ("wg", 1, 2, 0), ("r3", 1, 0, 1), ("r2", 1, 0, 4),
+    ("r1", 1, 1, 3), ("r1", 1, 1, 5), ("r5", 0, 0, 7), ("r5", 0, 1, 6), ("r1", 1, 0, 6), ("r4", 0, 1, 5),
+    ("r5", 0, 0, 5), ("r1", 1, 1, 6), ("r4", 0, 1, 7), ("r1", 1, 0, 5), ("r5", 0, 1, 4), ("r1", 1, 0, 2),
+    ("r4", 1, 0, 1), ("r1", 1, 0, 7), ("r1", 1, 1, 7), ("r2", 1, 1, 5), ("r2", 1, 0, 6), ("r5", 0, 1, 5),
+    ("wg", 1, 2, 2), ("r2", 1, 1, 6), ("r2", 1, 0, 5), ("r5", 0, 1, 7), ("wg", 1, 2, 3), ("r3", 1, 0, 7),
+    ("r5", 1, 0, 1), ("wg", 0, 0, 0), ("r3", 1, 1, 7), ("r5", 0, 1, 2), ("wg", 1, 2, 1), ("r3", 1, 0, 6),
+    ("r3", 1, 1, 6), ("cs", 1, 1), ("r3", 1, 1, 5), ("r3", 1, 0, 5), ("cs", 1, 0), ("r3", 1, 0, 4),
+    ("r5", 1, 0, 7), ("r2", 1, 1, 4), ("r2", 1, 0, 3), ("r2", 1, 1, 3), ("r2", 1, 0, 2), ("fs", 1, 1),
+    ("r5", 1, 1, 7), ("ip", 7), ("ss", 0, 0, 0), ("r4", 1, 0, 6), ("fs", 1, 0), ("ss", 1, 0, 1),
+    ("r4", 1, 1, 6), ("bp", 7), ("r1", 1, 1, 2), ("r4", 1, 0, 5), ("r4", 1, 1, 5), ("r1", 1, 1, 1),
+    ("r1", 1, 1, 0), ("r3", 1, 1, 4), ("r3", 1, 0, 3), ("r4", 1, 0, 4), ("r3", 1, 1, 3), ("r3", 1, 0, 2),
+    ("r5", 1, 0, 6), ("wg", 0, 0, 3), ("r5", 1, 1, 6), ("ip", 6), ("ss", 0, 1, 1), ("r5", 1, 0, 5),
+    ("r2", 1, 1, 2), ("r5", 1, 1, 5), ("ip", 5), ("ss", 1, 1, 0), ("ss", 1, 1, 1), ("r2", 1, 1, 1),
+    ("r4", 1, 1, 4), ("wg", 0, 1, 3), ("r4", 1, 0, 3), ("bp", 5), ("wo", 1, 1), ("bp", 6), ("r4", 1, 1, 3),
+    ("r2", 1, 1, 0), ("r5", 1, 0, 4), ("ss", 0, 1, 0), ("r4", 1, 0, 2), ("wg", 0, 0, 2), ("r3", 1, 1, 2),
+    ("r3", 1, 1, 1), ("r5", 1, 1, 4), ("ip", 4), ("ss", 0, 2, 1), ("bp", 4), ("r5", 1, 1, 3),
+    ("r5", 1, 0, 3), ("ip", 3), ("ss", 1, 2, 0), ("r3", 1, 1, 0), ("r5", 1, 0, 2), ("wg", 0, 0, 1),
+    ("r4", 1, 1, 2), ("bp", 3), ("cs", 0, 0), ("wo", 1, 0), ("r4", 1, 1, 1), ("wg", 0, 1, 2),
+    ("ss", 0, 2, 0), ("ss", 1, 2, 1), ("fs", 0, 0), ("r4", 1, 1, 0), ("r5", 1, 1, 2), ("ip", 2), ("bp", 2),
+    ("wg", 0, 1, 1), ("ss", 0, 3, 1), ("r5", 1, 1, 1), ("ip", 1), ("bp", 1), ("ss", 1, 3, 0),
+    ("r5", 1, 1, 0), ("bp", 0), ("bc",), ("wg", 0, 1, 0), ("cs", 0, 1), ("ip", 0), ("bf",), ("ss", 0, 3, 0),
+    ("ss", 1, 3, 1), ("fs", 0, 1), ("wo", 0, 0), ("bo",), ("yb",), ("wo", 0, 1), ("io",),
 )
 
 
@@ -143,6 +145,11 @@
     def held_rows(which, of):
         size = PARTS[of][1]
         return span(PLACE[of] + which * size, size, 16)
+
+    barrier = pltpu.get_barrier_semaphore()
+    everyone = [x_right, x_left, x_across, z_right, z_left, core] + [p[2] for p in y_peers]
+    for device in everyone:
+        pl.semaphore_signal(barrier, inc=1, device_id=device, device_id_type=MESH)
 
     own = {}
     for j, (block, weights, held) in enumerate(((tok, win, wi), (og, wout, wo))):
@@ -183,10 +190,6 @@
     for held in (wi, wo):
         held[pl.ds(HID, PADDED - HID)] = jnp.zeros((PADDED - HID, WIDE), BF16)
 
-    barrier = pltpu.get_barrier_semaphore()
-    everyone = [x_right, x_left, x_across, z_right, z_left, core] + [p[2] for p in y_peers]
-    for device in everyone:
-        pl.semaphore_signal(barrier, inc=1, device_id=device, device_id_type=MESH)
     pl.semaphore_wait(barrier, len(everyone))
 
     spread, weight_far, weight_core, ring = {}, {}, {}, {}
@@ -335,7 +338,12 @@
                 0.5 * (1.0 + bend) + 0.5 * value * (1.0 - bend * bend) * slope
             )
         ap[j, slot, mine, at_lanes] = result.astype(BF16)
-        block = ap.at[j, slot, mine, at_lanes]
+        if j == 1:
+            hand_out(j, lanes, slot)
+
+    def hand_out(j, lanes, slot):
+        block = ap.at[j, slot, quarter(0), pl.ds(*LANES[lanes])]
+        direct = (j, lanes, slot) in DIRECT
         others = [x_across] * direct + [x_right, x_left]
         stage[4 if direct else 3, j, lanes, slot] = [
             send(block, block, device) for device in others
@@ -460,7 +468,7 @@
 
     steps = {
         "sx": begin, "zs": ring_start, "zf": ring_pass, "wf": weights_pass,
-        "r1": multiply, "r2": add_first, "r3": activate, "r4": hand_on, "r5": all_here,
+        "r1": multiply, "r2": add_first, "r3": activate, "ra": hand_out, "r4": hand_on, "r5": all_here,
         "wg": weight_grad, "cs": core_send, "fs": far_send, "wo": weight_out,
         "bp": bias_part, "bc": bias_core, "bf": bias_far, "bo": bias_out,
         "ip": input_part, "ss": sum_pass, "yb": sum_end, "io": input_out,

time: 128 us -> 127 us (level)
    pallas_call x1, Pallas kernels: 126 us -> 125 us  [local(): pl.pallas_call(kernel, name='ffn_backward', out_shape=(pltpu.VMEM((GROUP,...]
where the time goes in v4:
time: 127 us
  Pallas kernels  126 us (99%)
    pallas_call x1, Pallas kernels, local(): pl.pallas_call(kernel, name='ffn_backward', out_shape=(pltpu.VMEM((GROUP,...  125 us

profile of v4, /device:TPU:1, one launch (start us, length us, event | category | flops | bytes accessed | tf_op | source)
XLA Modules:
  0.0 126.9 jit_solution(2055797218588771039)
XLA Ops:
  0.6 125.0 %ffn_backward.1 = (bf16[128,640]{1,0:T(8,128)(2,1)S(1)}, bf16[432,640]{1,0:T(8,128)(2,1)S(1)}, f32[1,432]{1,0:T(1,128)S(1)}, bf16[432,640]{1,0:T(8,128)(2,1)S(1)}) custom-call(bf16[128,640]{1,0:T(8,128)(2,1)} %tok.1, bf16[128,640]{1,0:T(8,128)(2,1)} %og.1, bf16[864,640]{1,0:T(8,128)(2,1)} %bitcast.3, f32[864]{0:T(1024)} %bias.1, bf16[864,640]{1,0:T(8,128)(2,1)} %wout.1), custom_call_target="tpu_custom_call" | custom-call | flops 11299999744 | bytes 4000000 | tf_op jit(solution)/shard_map/ffn_backward/pallas_call | solution.py:494
  125.7 1.1 hand_over.1

commit v5 on v4

--- a/solution.py
+++ b/solution.py
@@ -96,9 +96,9 @@
     core = at(rep_=1 - rep)
     y_far = at(yh_=1 - yh)
     y_peers = [
-        (yh, 1 - yl, at(yl_=1 - yl)),
         (1 - yh, yl, y_far),
         (1 - yh, 1 - yl, at(yh_=1 - yh, yl_=1 - yl)),
+        (yh, 1 - yl, at(yl_=1 - yl)),
     ]
 
     counts = {"local": 0, "remote": 0}

time: 127 us -> 123 us (0.969)
  Pallas kernels: 126 us -> 122 us
    pallas_call x1, Pallas kernels: 125 us -> 121 us  [local(): pl.pallas_call(kernel, name='ffn_backward', out_shape=(pltpu.VMEM((GROUP,...]
where the time goes in v5:
time: 123 us
  Pallas kernels  122 us (99%)
    pallas_call x1, Pallas kernels, local(): pl.pallas_call(kernel, name='ffn_backward', out_shape=(pltpu.VMEM((GROUP,...  121 us

profile of v5, /device:TPU:1, one launch (start us, length us, event | category | flops | bytes accessed | tf_op | source)
XLA Modules:
  0.0 122.8 jit_solution(6984162100808069957)
XLA Ops:
  0.6 120.9 %ffn_backward.1 = (bf16[128,640]{1,0:T(8,128)(2,1)S(1)}, bf16[432,640]{1,0:T(8,128)(2,1)S(1)}, f32[1,432]{1,0:T(1,128)S(1)}, bf16[432,640]{1,0:T(8,128)(2,1)S(1)}) custom-call(bf16[128,640]{1,0:T(8,128)(2,1)} %tok.1, bf16[128,640]{1,0:T(8,128)(2,1)} %og.1, bf16[864,640]{1,0:T(8,128)(2,1)} %bitcast.3, f32[864]{0:T(1024)} %bias.1, bf16[864,640]{1,0:T(8,128)(2,1)} %wout.1), custom_call_target="tpu_custom_call" | custom-call | flops 11299999744 | bytes 4000000 | tf_op jit(solution)/shard_map/ffn_backward/pallas_call | solution.py:494
  121.5 1.1 hand_over.1
